TPU v7x, 32 devices: a whole 2x2x4 slice. The times are simulated.
32 devices in a mesh: pipe: 4 (over z), dp: 8 (over y, x, core).
Axes of the slice: x: 2, y: 2, z: 4, core: 2. Of those that a mesh axis runs over, the one named last changes fastest.
Arguments:
- fwd_latents: bfloat16 [4, 6656, 1024], P('pipe', 'dp'), may hold values from -6 to 6
- fwd_segments: int32 [4, 6656], P('pipe', 'dp'), may hold values from 0 to 3, as said below
- stash_latents: bfloat16 [4, 6656, 1024], P('pipe', 'dp'), may hold values from -6 to 6
- stash_segments: int32 [4, 6656], P('pipe', 'dp'), may hold values from 0 to 3, as said below
- upstream_grad: bfloat16 [4, 6656, 1024], P('pipe', 'dp'), may hold values from -6 to 6
- qkv_weight: bfloat16 [3, 1024, 1024], P(None, 'dp'), may hold values from -0.1875 to 0.1875
- out_weight: bfloat16 [1024, 1024], P('dp'), may hold values from -3 to 3
- mlp_weight: bfloat16 [2, 1024, 1024], P(None, 'dp'), may hold values from -0.1875 to 0.1875
- norm_gain: bfloat16 [2, 1024], P(None, 'dp'), may hold values from 0.5 to 1.5
- biases: bfloat16 [7, 1024], P(None, 'dp'), may hold values from -1.5 to 1.5
Outputs:
- latents: bfloat16 [4, 6656, 1024], P('pipe', 'dp')
- input_grad: bfloat16 [4, 6656, 1024], P('pipe', 'dp')
- qkv_grad: float32 [3, 1024, 1024], P(None, 'dp')
- out_grad: float32 [1024, 1024], P('dp')
- mlp_grad: float32 [2, 1024, 1024], P(None, 'dp')
- gain_grad: float32 [2, 1024], P(None, 'dp')
- bias_grad: float32 [7, 1024], P(None, 'dp')
- shift_grad: float32 [1024], P('dp')
Inputs may be any that keep to these rules, and one draw needn't show every extreme that they name: `fwd_segments`: in each device's 832 slots of a section, ids never fall; each of 0, 1, 2 that occurs marks one image of 256, 512 or 832 slots, and 3 marks the empty slots at the end. In every section one device holds one image of 832 slots and another has empty slots. `stash_segments`: as for fwd_segments.
All inputs are finite; a program needn't handle non-finite values.
Results may differ from a plain program's by a relative error of at most 0.017.
Values may be sent and summed in bfloat16 or wider, within the bound.
No kernel may reach another device: no remote copies, remote signals or barrier semaphores. Data moves between devices by JAX's collectives and lax.ppermute only.
A program may use at most 256 MiB of HBM per device.

v0:
```python
import jax
import jax.numpy as jnp
from jax import lax
from jax.sharding import PartitionSpec as P

HEADS = 8
HEAD = 128


EPSILON = 1e-05


def shifted(value, axis, steps):
    count = lax.axis_size(axis)
    pairs = [(source, (source + steps) % count) for source in range(count)]
    return lax.ppermute(value, axis, pairs)


def norm_rows(latent_rows, gain_row, shift_row):
    row_mean = jnp.mean(latent_rows, axis=-1, keepdims=True)
    centred = latent_rows - row_mean
    spread = jnp.mean(centred * centred, axis=-1, keepdims=True)
    return centred * lax.rsqrt(spread + EPSILON) * gain_row + shift_row


def head_major(matrix):
    return matrix.reshape(matrix.shape[0], HEADS, HEAD).transpose(1, 0, 2)


def row_major(stacked):
    return stacked.transpose(1, 0, 2).reshape(stacked.shape[1], HEADS * HEAD)


def masked_scores(queries, key_rows, same_image):
    scores = jnp.einsum(
        "qd,kd->qk", queries, key_rows, preferred_element_type=jnp.float32
    ) * HEAD ** (-0.5)
    return jnp.where(same_image, scores, -1e30)


def head_forward(queries, key_rows, values, same_image):
    scores = masked_scores(queries, key_rows, same_image)
    row_top = jnp.max(scores, axis=-1, keepdims=True)
    exponent = jnp.exp(scores - row_top)
    row_total = jnp.sum(exponent, axis=-1, keepdims=True)
    weights = (exponent / row_total).astype(jnp.bfloat16)
    mixed_rows = jnp.dot(weights, values, preferred_element_type=jnp.float32)
    return (mixed_rows.astype(jnp.bfloat16), (row_top + jnp.log(row_total))[:, 0])


def head_backward(queries, key_rows, values, log_total, dmixed, same_image):
    scores = masked_scores(queries, key_rows, same_image)
    probs = jnp.exp(scores - log_total[:, None])
    weights = probs.astype(jnp.bfloat16)
    dprobs = jnp.einsum("qd,kd->qk", dmixed, values, preferred_element_type=jnp.float32)
    dvalues = jnp.einsum("qk,qd->kd", weights, dmixed, preferred_element_type=jnp.float32)
    dscores = (probs * (dprobs - jnp.sum(dprobs * probs, axis=-1, keepdims=True))).astype(
        jnp.bfloat16
    )
    dqueries = jnp.dot(dscores, key_rows, preferred_element_type=jnp.float32) * HEAD ** (-0.5)
    dkeys = jnp.einsum(
        "qk,qd->kd", dscores, queries, preferred_element_type=jnp.float32
    ) * HEAD ** (-0.5)
    return (dqueries.astype(jnp.bfloat16), dkeys.astype(jnp.bfloat16), dvalues.astype(jnp.bfloat16))


def layer_forward(params, latents_in, segment_ids):
    qkv_w, out_w, mlp_w, gains, shifts = params
    gain_rows = gains.astype(jnp.float32)
    shift_rows = shifts.astype(jnp.float32)
    latent_rows = latents_in.astype(jnp.float32)
    normed = norm_rows(latent_rows, gain_rows[0], shift_rows[0]).astype(jnp.bfloat16)
    projected = jnp.einsum("td,sde->ste", normed, qkv_w, preferred_element_type=jnp.float32)
    queries = (projected[0] + shift_rows[1]).astype(jnp.bfloat16)
    key_rows = projected[1].astype(jnp.bfloat16)
    values = (projected[2] + shift_rows[2]).astype(jnp.bfloat16)
    same_image = segment_ids[:, None] == segment_ids[None, :]
    mixed_heads, log_total = lax.map(
        lambda triple: head_forward(triple[0], triple[1], triple[2], same_image),
        (head_major(queries), head_major(key_rows), head_major(values)),
    )
    mixed_rows = row_major(mixed_heads)
    attended = (
        latent_rows + jnp.dot(mixed_rows, out_w, preferred_element_type=jnp.float32) + shift_rows[3]
    )
    normed2 = norm_rows(attended, gain_rows[1], shift_rows[4]).astype(jnp.bfloat16)
    hidden = jnp.dot(normed2, mlp_w[0], preferred_element_type=jnp.float32) + shift_rows[5]
    active = jax.nn.gelu(hidden).astype(jnp.bfloat16)
    return {
        "latent_rows": latent_rows,
        "normed": normed,
        "queries": queries,
        "key_rows": key_rows,
        "values": values,
        "same_image": same_image,
        "log_total": log_total,
        "mixed_rows": mixed_rows,
        "attended": attended,
        "normed2": normed2,
        "hidden": hidden,
        "active": active,
        "gain_rows": gain_rows,
        "shift_rows": shift_rows,
    }


def layer_backward(params, latents_in, segment_ids, grad_out):
    qkv_w, out_w, mlp_w, gains, shifts = params
    stored = layer_forward(params, latents_in, segment_ids)
    gain_rows = stored["gain_rows"]
    shift_rows = stored["shift_rows"]
    dout = grad_out.astype(jnp.bfloat16)
    bias_last = jnp.sum(dout.astype(jnp.float32), axis=0)
    grad_second = jnp.einsum(
        "tf,te->fe", stored["active"], dout, preferred_element_type=jnp.float32
    )
    dactive = jnp.einsum("te,fe->tf", dout, mlp_w[1], preferred_element_type=jnp.float32)
    _, gelu_pull = jax.vjp(jax.nn.gelu, stored["hidden"])
    dhidden = gelu_pull(dactive)[0].astype(jnp.bfloat16)
    bias_hidden = jnp.sum(dhidden.astype(jnp.float32), axis=0)
    grad_first = jnp.einsum(
        "td,tf->df", stored["normed2"], dhidden, preferred_element_type=jnp.float32
    )
    dnormed2 = jnp.einsum("tf,df->td", dhidden, mlp_w[0], preferred_element_type=jnp.float32)
    _, second_pull = jax.vjp(norm_rows, stored["attended"], gain_rows[1], shift_rows[4])
    dattended_norm, dgain_second, dshift_second = second_pull(dnormed2)
    dattended = grad_out + dattended_norm
    dattn = dattended.astype(jnp.bfloat16)
    bias_out = jnp.sum(dattn.astype(jnp.float32), axis=0)
    grad_out_w = jnp.einsum(
        "td,te->de", stored["mixed_rows"], dattn, preferred_element_type=jnp.float32
    )
    dmixed = jnp.einsum("te,de->td", dattn, out_w, preferred_element_type=jnp.float32).astype(
        jnp.bfloat16
    )
    same_image = stored["same_image"]
    dqueries, dkeys, dvalues = lax.map(
        lambda quintet: head_backward(
            quintet[0], quintet[1], quintet[2], quintet[3], quintet[4], same_image
        ),
        (
            head_major(stored["queries"]),
            head_major(stored["key_rows"]),
            head_major(stored["values"]),
            stored["log_total"],
            head_major(dmixed),
        ),
    )
    dprojected = jnp.stack([row_major(dqueries), row_major(dkeys), row_major(dvalues)])
    bias_query = jnp.sum(dprojected[0].astype(jnp.float32), axis=0)
    bias_value = jnp.sum(dprojected[2].astype(jnp.float32), axis=0)
    grad_qkv = jnp.einsum(
        "td,ste->sde", stored["normed"], dprojected, preferred_element_type=jnp.float32
    )
    dnormed = jnp.einsum("ste,sde->td", dprojected, qkv_w, preferred_element_type=jnp.float32)
    _, first_pull = jax.vjp(norm_rows, stored["latent_rows"], gain_rows[0], shift_rows[0])
    drows, dgain_first, dshift_first = first_pull(dnormed)
    dlatents = (dattended + drows).astype(jnp.bfloat16)
    gain_terms = jnp.stack([dgain_first, dgain_second])
    bias_terms = jnp.stack(
        [dshift_first, bias_query, bias_value, bias_out, dshift_second, bias_hidden, bias_last]
    )
    return (
        dlatents,
        (grad_qkv, grad_out_w, jnp.stack([grad_first, grad_second]), gain_terms, bias_terms),
    )


def local(
    fwd_latents,
    fwd_segments,
    stash_latents,
    stash_segments,
    upstream_grad,
    qkv_weight,
    out_weight,
    mlp_weight,
    norm_gain,
    biases,
):
    arriving = shifted(upstream_grad, "pipe", -1)
    params = (
        lax.all_gather(qkv_weight, "dp", axis=1, tiled=True),
        lax.all_gather(out_weight, "dp", axis=0, tiled=True),
        lax.all_gather(mlp_weight, "dp", axis=1, tiled=True),
        lax.all_gather(norm_gain, "dp", axis=1, tiled=True),
        lax.all_gather(biases, "dp", axis=1, tiled=True),
    )
    stored = layer_forward(params, fwd_latents[0], fwd_segments[0])
    output = (
        stored["attended"]
        + jnp.dot(stored["active"], params[2][1], preferred_element_type=jnp.float32)
        + stored["shift_rows"][6]
    )
    live_rows = (fwd_segments[0] < 3)[:, None]
    result = jnp.where(live_rows, output, 0.0).astype(jnp.bfloat16)
    latents = shifted(result[None], "pipe", 1)
    stash_live = (stash_segments[0] < 3)[:, None]
    grad_out = jnp.where(stash_live, arriving[0].astype(jnp.float32), 0.0)
    dlatents, grad_terms = layer_backward(params, stash_latents[0], stash_segments[0], grad_out)
    grad_parts = (
        lax.psum_scatter(
            grad_terms[0].astype(jnp.bfloat16), "dp", scatter_dimension=1, tiled=True
        ).astype(jnp.float32),
        lax.psum_scatter(
            grad_terms[1].astype(jnp.bfloat16), "dp", scatter_dimension=0, tiled=True
        ).astype(jnp.float32),
        lax.psum_scatter(
            grad_terms[2].astype(jnp.bfloat16), "dp", scatter_dimension=1, tiled=True
        ).astype(jnp.float32),
        lax.psum_scatter(
            grad_terms[3].astype(jnp.bfloat16), "dp", scatter_dimension=1, tiled=True
        ).astype(jnp.float32),
        lax.psum_scatter(
            grad_terms[4].astype(jnp.bfloat16), "dp", scatter_dimension=1, tiled=True
        ).astype(jnp.float32),
    )
    totals = (
        lax.psum(grad_parts[0].astype(jnp.bfloat16), "pipe").astype(jnp.float32),
        lax.psum(grad_parts[1].astype(jnp.bfloat16), "pipe").astype(jnp.float32),
        lax.psum(grad_parts[2].astype(jnp.bfloat16), "pipe").astype(jnp.float32),
        lax.psum(grad_parts[3].astype(jnp.bfloat16), "pipe").astype(jnp.float32),
        lax.psum(grad_parts[4].astype(jnp.bfloat16), "pipe").astype(jnp.float32),
    )
    return (
        latents,
        dlatents[None],
        totals[0],
        totals[1],
        totals[2],
        totals[3],
        totals[4],
        totals[4][4],
    )


def solution(mesh):
    in_specs = (
        P("pipe", "dp", None),
        P("pipe", "dp"),
        P("pipe", "dp", None),
        P("pipe", "dp"),
        P("pipe", "dp", None),
        P(None, "dp", None),
        P("dp", None),
        P(None, "dp", None),
        P(None, "dp"),
        P(None, "dp"),
    )
    out_specs = (
        P("pipe", "dp", None),
        P("pipe", "dp", None),
        P(None, "dp", None),
        P("dp", None),
        P(None, "dp", None),
        P(None, "dp"),
        P(None, "dp"),
        P("dp"),
    )
    return jax.shard_map(local, mesh=mesh, in_specs=in_specs, out_specs=out_specs, check_vma=False)
```

profile of v0, /device:TPU:0, one launch (start us, length us, event | category | flops | bytes accessed | tf_op | source)
XLA Modules:
  0.0 627.0 jit_solution(18350385113626432639)
XLA Ops:
  8.7 5.1 collective-permute-start.1
  14.6 8.9 %all_gather.15 = bf16[2,1024]{1,0:T(2,128)(2,1)S(1)} all-gather(bf16[2,128]{1,0:T(2,128)(2,1)} %param.24), channel_id=1, replica_groups=mesh['pipe'=4,'dp'=8] {'dp'}, dimensions={1}, use_global_device_ids=true | all-gather | bytes 4608 | tf_op jit(solution)/shard_map/all_gather | solution.py:186
  27.5 8.8 %all_gather.16 = bf16[7,1024]{1,0:T(8,128)(2,1)S(1)} all-gather(bf16[7,128]{1,0:T(8,128)(2,1)S(1)} %copy-done.34), channel_id=1, replica_groups=mesh['pipe'=4,'dp'=8] {'dp'}, dimensions={1}, use_global_device_ids=true | all-gather | bytes 16128 | tf_op jit(solution)/shard_map/all_gather | solution.py:187
  36.9 21.4 %all-gather.4.cloned.1.call-done = bf16[3,1024,1024]{2,1,0:T(8,128)(2,1)} async-done(((bf16[3,128,1024]{2,1,0:T(8,128)(2,1)}), bf16[3,1024,1024]{2,1,0:T(8,128)(2,1)}) %all-gather.4.cloned.1.call-update) | async-done | bytes 6291472 | tf_op jit(solution)/shard_map/all_gather | solution.py:183
  58.2 7.9 %convolution_bitcast_fusion = f32[3,832,1024]{2,1,0:T(8,128)S(1)} fusion(bf16[3,1024,1024]{2,1,0:T(8,128)(2,1)} %all-gather.4.cloned.1.call-done, bf16[1,832,1024]{2,1,0:T(8,128)(2,1)S(1)} %copy-done.2, f32[832]{0:T(1024)S(1)} %fusion.165, f32[832]{0:T(1024)S(1)} %broadcast_multiply_fusion.1, f32[1024]{0:T(1024)S(1)} %bitcast.411, f32[1024]{0:T(1024)S(1)} %bitcast.383), kind=kOutput, calls=%fused_computation.106 | convolution fusion | flops 5239603200 | bytes 18233856 | tf_op jit(solution)/shard_map/td,sde->ste/dot_general | solution.py:73
  67.8 11.2 %convolution_bitcast_fusion.1 = f32[3,832,1024]{2,1,0:T(8,128)} fusion(bf16[3,1024,1024]{2,1,0:T(8,128)(2,1)} %all-gather.4.cloned.1.call-done, bf16[1,832,1024]{2,1,0:T(8,128)(2,1)S(1)} %copy-done.9, f32[1024]{0:T(1024)S(1)} %bitcast.412, f32[1024]{0:T(1024)S(1)} %bitcast.384, f32[832]{0:T(1024)S(1)} %add_rsqrt_fusion.1, f32[832]{0:T(1024)S(1)} %broadcast_multiply_fusion.3), kind=kOutput, calls=%fused_computation.107 | convolution fusion | flops 5239603200 | bytes 18233856 | tf_op jit(solution)/shard_map/td,sde->ste/dot_general | solution.py:73
  79.0 3.6 slice_bitcast_fusion.2
  87.9 5.3 fusion.130
  94.6 35.3 %while.40 = (s32[]{:T(128)}, bf16[8,832,128]{2,1,0:T(8,128)(2,1)}, f32[8,832]{1,0:T(8,128)S(1)}, bf16[8,832,128]{2,1,0:T(8,128)(2,1)}, bf16[8,832,128]{2,1,0:T(8...) while((s32[]{:T(128)}, bf16[8,832,128]{2,1,0:T(8,128)(2,1)}, ...), condition=%wide.region_13.14_spmd.clone, body=%wide.region_10.13_spmd.clone.sunk | while | flops 364907712 | bytes 9434985 | solution.py:78
  129.9 4.8 fusion.186
  136.9 4.8 fusion.159
  141.7 7.3 %fusion.187 = (bf16[1024]{0:T(1024)(128)(2,1)}, bf16[832,1024]{1,0:T(8,128)(2,1)S(1)}) fusion(f32[832,1024]{1,0:T(8,128)S(1)} %fusion.159, f32[1024]{0:T(1024)S(1)} %bitcast.405, bf16[2,1024,1024]{2,1,0:T(8,128)(2,1)S(1)} %copy-done.37, bf16[1,832,1024]{2,1,0:T(8,128)(2,1)} %collective-permute-done.1, pred[832]{0:T(1024)(128)(4,1)S(1)} %broadcast_compare_fusion), kind=kOutput, calls=%fused_computation.253 | convolution fusion | flops 1766128640 | bytes 8920064 | tf_op jit(solution)/shard_map/te,fe->tf/dot_general | solution.py:117
  149.0 3.1 multiply_reduce_fusion.1
  153.2 4.0 fusion.180
  163.7 78.4 %while.41 = (s32[]{:T(128)}, bf16[8,832,128]{2,1,0:T(8,128)(2,1)S(1)}, bf16[8,832,128]{2,1,0:T(8,128)(2,1)}, bf16[8,832,128]{2,1,0:T(8,128)(2,1)}, bf16[8,832,12...) while((s32[]{:T(128)}, ...), condition=%wide.region_20.21_spmd.clone, body=%wide.region_18.20_spmd.clone.sunk | while | flops 893500608 | bytes 23033976 | solution.py:137
  242.1 4.4 copy.52
  246.4 3.8 stack_reshape.10
  252.5 3.8 stack_reshape.9
  256.2 3.7 copy.53
  260.0 3.8 stack_reshape.11
  268.7 9.5 %convert_bitcast_fusion = bf16[3,1024,1024]{1,2,0:T(8,128)(2,1)} fusion(bf16[3,832,1024]{2,1,0:T(8,128)(2,1)S(1)} %constant_dynamic-update-slice_fusion, bf16[1,832,1024]{2,1,0:T(8,128)(2,1)S(1)} %copy-done.2, f32[832]{0:T(1024)S(1)} %copy-done.24, f32[832]{0:T(1024)S(1)} %copy-done.20, f32[1024]{0:T(1024)S(1)} %bitcast.413, f32[1024]{0:T(1024)S(1)} %bitcast.385), kind=kOutput, calls=%fused_computation.81 | convolution fusion | flops 5242748928 | bytes 13122048 | tf_op jit(solution)/shard_map/td,ste->sde/dot_general | solution.py:152
  278.2 14.3 %copy.55 = bf16[3,1024,1024]{2,0,1:T(4,128)(2,1)} copy(bf16[3,1024,1024]{1,2,0:T(8,128)(2,1)} %convert_bitcast_fusion) | data formatting | bytes 12582912
  292.6 10.2 %copy.70 = bf16[128,8,3,1024]{3,1,2,0:T(8,128)(2,1)} copy(bf16[128,8,3,1024]{3,2,1,0:T(4,128)(2,1)} %bitcast.366) | data formatting | bytes 12582912
  304.2 5.1 convolution_convert_fusion
  309.4 2.6 fusion.132
  315.8 2.7 convert_bitcast_fusion.5
  318.6 4.4 convert_bitcast_fusion.4
  327.0 42.2 %while.39 = (s32[]{:T(128)}, bf16[8,832,128]{2,1,0:T(8,128)(2,1)}, bf16[8,832,128]{2,1,0:T(8,128)(2,1)}, bf16[8,832,128]{2,1,0:T(8,128)(2,1)}, bf16[8,832,128]{2,1,0:T(8,128)(2,1)}, /*index=5*/s32[832]{0:T(1024)S(1)}, s32[]{:T(128)}) while((s32[]{:T(128)}, bf16[8,832,128]{2,1,0:T(8,128)(2,1)}, bf16[8,832,128]{2,1,0:T(8,128)(2,1)}, ...), condition=%wide.region_5.6_spmd.clone, body=%wide.region_2.5_spmd.clone.sunk | while | flops 364906880 | bytes 9411669 | solution.py:78
  329.8 2.8 fusion.227
  335.0 2.8 fusion.227
  340.2 2.8 fusion.227
  345.5 2.8 fusion.227
  350.7 2.8 fusion.227
  355.9 2.8 fusion.227
  361.2 2.8 fusion.227
  366.4 2.8 fusion.227
  369.2 4.2 fusion.185
  375.7 9.4 %fusion.126 = bf16[1,832,1024]{2,1,0:T(8,128)(2,1)} fusion(f32[832,1024]{1,0:T(8,128)} %copy-done.14, f32[1024]{0:T(1024)S(1)} %bitcast.408, pred[832]{0:T(1024)(128)(4,1)S(1)} %broadcast_compare_fusion.1, bf16[2,1024,1024]{2,1,0:T(8,128)(2,1)} %all-gather.8.cloned.1.call-done, f32[1024]{0:T(1024)S(1)} %bitcast.407, f32[1024]{0:T(1024)S(1)} %bitcast.404, ...), kind=kOutput, calls=%fused_computation.172 | convolution fusion | flops 3505848320 | bytes 12737856 | tf_op jit(solution)/shard_map/dot_general | solution.py:192
  386.5 9.5 %bitcast_reduce_fusion = (bf16[1024]{0:T(1024)(128)(2,1)S(1)}, f32[832]{0:T(1024)S(1)}, f32[832,1024,1]{1,0,2:T(8,128)S(1)}) fusion(f32[1024]{0:T(1024)S(1)} %bitcast.386, f32[832]{0:T(1024)S(1)} %copy-done.20, bf16[1,832,1024]{2,1,0:T(8,128)(2,1)S(1)} %copy-done.2, bf16[3,832,1024]{2,1,0:T(8,128)(2,1)} %copy-done.17, ...), kind=kOutput, calls=%fused_computation.144 | convolution fusion | flops 5239601152 | bytes 16527872 | tf_op jit(solution)/shard_map/ste,sde->td/dot_general | solution.py:155
  402.4 3.6 reshape.222
  410.0 54.6 %reduce-scatter.14.cloned.1.call-done = bf16[2,128,1024]{2,1,0:T(8,128)(2,1)} async-done(((bf16[2,1024,1024]{2,1,0:T(8,128)(2,1)}), bf16[2,128,1024]{2,1,0:T(8,128)(2,1)}) %reduce-scatter.14.cloned.1.call-update) | async-done | bytes 524304 | tf_op jit(solution)/shard_map/reduce_scatter | solution.py:208
  464.7 4.8 fusion.127
  469.5 32.7 %reduce-scatter.18.cloned.1.call-done = bf16[128,2]{1,0:T(8,128)(2,1)} async-done(((bf16[1024,2]{1,0:T(8,128)(2,1)}), bf16[128,2]{1,0:T(8,128)(2,1)}) %reduce-scatter.18.cloned.1.call-update) | async-done | bytes 528
  503.0 35.9 %reduce-scatter.20.cloned.1.call-done = bf16[128,7]{1,0:T(8,128)(2,1)} async-done(((bf16[1024,7]{1,0:T(8,128)(2,1)}), bf16[128,7]{1,0:T(8,128)(2,1)}) %reduce-scatter.20.cloned.1.call-update) | async-done | bytes 1808
  539.6 11.8 %all-reduce = (bf16[2,128]{1,0:T(2,128)(2,1)S(1)}, bf16[7,128]{1,0:T(8,128)(2,1)S(1)}) all-reduce(bf16[2,128]{1,0:T(2,128)(2,1)S(1)} %copy.58, bf16[7,128]{1,0:T(8,128)(2,1)S(1)} %copy.60), channel_id=1, replica_groups=mesh['pipe'=4,'dp'=8] {'pipe'}, use_global_device_ids=true, to_apply=%region_32.33 | all-reduce | flops 1152 | bytes 4608 | tf_op jit(solution)/shard_map/psum | solution.py:222
  552.6 59.5 %all-reduce.4.cloned.1.call-done = (bf16[3,128,1024]{1,2,0:T(8,128)(2,1)}, bf16[128,1024]{1,0:T(8,128)(2,1)}, bf16[2,128,1024]{2,1,0:T(8,128)(2,1)}) async-done(((bf16[3,128,1024]{1,2,0:T(8,128)(2,1)}, bf16[128,1024]{1,0:T(8,128)(2,1)}, bf16[2,128,1024]{2,1,0:T(8,128)(2,1)}), (bf16[3,128,1024]{1,2,0:T(8,128)(2,1)}, bf16[128,1024]{1,0:T(8,128)(2,1)}, ...) | async-done | bytes 1572880 | tf_op jit(solution)/shard_map/psum | solution.py:219
  613.9 2.5 copy.54
  617.5 2.8 copy.159
  (303 shorter events, 193.6 us)
Async XLA Ops:
  7.2 18.1 %copy-start.9 = (bf16[1,832,1024]{2,1,0:T(8,128)(2,1)S(1)}, bf16[1,832,1024]{2,1,0:T(8,128)(2,1)}, u32[]{:S(2)}) copy-start(bf16[1,832,1024]{2,1,0:T(8,128)(2,1)} %param.16) | copy-start | bytes 5111812
  7.2 18.7 %copy-start.2 = (bf16[1,832,1024]{2,1,0:T(8,128)(2,1)S(1)}, bf16[1,832,1024]{2,1,0:T(8,128)(2,1)}, u32[]{:S(2)}) copy-start(bf16[1,832,1024]{2,1,0:T(8,128)(2,1)} %param.18) | copy-start | bytes 5111812
  7.2 51.0 %all-gather.4.cloned.1.call-start = ((), (), s32[]{:S(2)}) async-start(), calls=%async_computation.5 | async-start | bytes 7077888 | tf_op jit(solution)/shard_map/all_gather | solution.py:183
  7.9 121.9 %all-gather.6.cloned.1.call-start = ((), (), s32[]{:S(2)}) async-start(), calls=%async_computation.6 | async-start | bytes 2359296 | tf_op jit(solution)/shard_map/all_gather | solution.py:184
  8.7 128.2 %all-gather.8.cloned.1.call-start = ((), (), s32[]{:S(2)}) async-start(), calls=%async_computation.7 | async-start | bytes 4718592 | tf_op jit(solution)/shard_map/all_gather | solution.py:185
  8.7 133.0 %collective-permute-start.1 = (bf16[1,832,1024]{2,1,0:T(8,128)(2,1)}, bf16[1,832,1024]{2,1,0:T(8,128)(2,1)}, u32[]{:S(2)}, u32[]{:S(2)}) collective-permute-start(bf16[1,832,1024]{2,1,0:T(8,128)(2,1)} %param.20), channel_id=1, source_target_pairs={{0,24},{8,0},{16,8},{24,16},{1,25},{9,1},{17,9},{25,17},{2,26},{10... | collective-permute-start | bytes 5111816 | tf_op jit(solution)/shard_map/ppermute | solution.py:16
  13.8 388.5 %reduce-scatter.16.cloned.1.call-start = ((), (), s32[]{:S(2)}) async-start(), calls=%async_computation.10 | async-start | bytes 7077888
  23.5 4.0 copy-start.34
  26.2 39.9 %copy-start.19 = (f32[832]{0:T(1024)}, f32[832]{0:T(1024)S(1)}, u32[]{:S(2)}) copy-start(f32[832]{0:T(1024)S(1)} %broadcast_multiply_fusion.1) | copy-start | bytes 9988
  27.4 38.7 %copy-start.23 = (f32[832]{0:T(1024)}, f32[832]{0:T(1024)S(1)}, u32[]{:S(2)}) copy-start(f32[832]{0:T(1024)S(1)} %fusion.165) | copy-start | bytes 9988
  36.9 93.0 %copy-start.30 = (f32[1,1024]{1,0:T(1,128)}, f32[1,1024]{1,0:T(1,128)S(1)}, u32[]{:S(2)}) copy-start(f32[1,1024]{1,0:T(1,128)S(1)} %get-tuple-element.293) | copy-start | bytes 12292
  129.8 4.8 copy-start.13
  136.9 4.8 copy-start.37
  141.7 7.3 %copy-start.39 = (f32[832,1024]{1,0:T(8,128)}, f32[832,1024]{1,0:T(8,128)S(1)}, u32[]{:S(2)}) copy-start(f32[832,1024]{1,0:T(8,128)S(1)} %fusion.159) | copy-start | bytes 10223620
  141.7 7.3 %copy-start.6 = (f32[832,1024]{1,0:T(8,128)S(1)}, f32[832,1024]{1,0:T(8,128)}, u32[]{:S(2)}) copy-start(f32[832,1024]{1,0:T(8,128)} %copy-done.5) | copy-start | bytes 10223620
  149.0 3.1 copy-start.41
  153.1 4.0 copy-start
  153.2 4.0 copy-start.25
  153.2 4.0 copy-start.38
  157.1 2.0 copy-start.16
  242.1 21.8 %copy-start.3 = (bf16[8,832,128]{2,1,0:T(8,128)(2,1)}, bf16[8,832,128]{2,1,0:T(8,128)(2,1)S(1)}, u32[]{:S(2)}) copy-start(bf16[8,832,128]{2,1,0:T(8,128)(2,1)S(1)} %get-tuple-element.135) | copy-start | bytes 5111812
  263.8 2.5 copy-start.12
  265.8 2.9 copy-start.20
  265.8 2.9 copy-start.24
  266.4 2.3 copy-start.17
  302.8 6.6 %copy-start.33 = (s32[1,832]{1,0:T(1,128)S(1)}, s32[1,832]{1,0:T(1,128)}, u32[]{:S(2)}) copy-start(s32[1,832]{1,0:T(1,128)} %param.17) | copy-start | bytes 9988
  302.8 107.3 %reduce-scatter.12.cloned.1.call-start = ((), (), s32[]{:S(2)}) async-start(), calls=%async_computation.8 | async-start | bytes 2359296 | tf_op jit(solution)/shard_map/reduce_scatter | solution.py:205
  309.3 155.3 %reduce-scatter.14.cloned.1.call-start = ((), (), s32[]{:S(2)}) async-start(), calls=%async_computation.9 | async-start | bytes 4718592 | tf_op jit(solution)/shard_map/reduce_scatter | solution.py:208
  312.0 3.1 copy-start.7
  312.0 3.8 copy-start.42
  315.8 2.8 copy-start.40
  325.4 176.8 %reduce-scatter.18.cloned.1.call-start = ((), (), s32[]{:S(2)}) async-start(), calls=%async_computation.11 | async-start | bytes 294912
  327.0 42.2 %copy-start.10 = (bf16[1,832,1024]{2,1,0:T(8,128)(2,1)S(1)}, bf16[1,832,1024]{2,1,0:T(8,128)(2,1)}, u32[]{:S(2)}) copy-start(bf16[1,832,1024]{2,1,0:T(8,128)(2,1)} %param.16) | copy-start | bytes 5111812
  327.0 42.2 %copy-start.31 = (f32[1,1024]{1,0:T(1,128)S(1)}, f32[1,1024]{1,0:T(1,128)}, u32[]{:S(2)}) copy-start(f32[1,1024]{1,0:T(1,128)} %copy-done.30) | copy-start | bytes 12292
  373.4 2.3 copy-start.29
  385.0 167.5 %collective-permute-start = (bf16[1,832,1024]{2,1,0:T(8,128)(2,1)}, bf16[1,832,1024]{2,1,0:T(8,128)(2,1)}, u32[]{:S(2)}, u32[]{:S(2)}) collective-permute-start(bf16[1,832,1024]{2,1,0:T(8,128)(2,1)} %fusion.126), channel_id=1, source_target_pairs={{0,8},{8,16},{16,24},{24,0},{1,9},{9,17},{17,25},{25,1},{2,10},{10... | collective-permute-start | bytes 5111816 | tf_op jit(solution)/shard_map/ppermute | solution.py:16
  386.5 9.6 %copy-start.22 = (f32[832]{0:T(1024)S(1)}, f32[832]{0:T(1024)}, u32[]{:S(2)}) copy-start(f32[832]{0:T(1024)} %copy-done.21) | copy-start | bytes 9988
  396.1 2.7 copy-start.4
  396.1 4.8 copy-start.35
  396.1 4.8 copy-start.36
  396.1 4.9 copy-start.28
  396.2 4.9 copy-start.27
  399.0 65.6 %copy-start.1 = (f32[832,1024]{1,0:T(8,128)S(1)}, f32[832,1024]{1,0:T(8,128)}, u32[]{:S(2)}) copy-start(f32[832,1024]{1,0:T(8,128)} %copy-done) | copy-start | bytes 10223620
  399.1 65.6 %copy-start.26 = (f32[832]{0:T(1024)S(1)}, f32[832]{0:T(1024)}, u32[]{:S(2)}) copy-start(f32[832]{0:T(1024)} %copy-done.25) | copy-start | bytes 9988
  399.1 139.7 %reduce-scatter.20.cloned.1.call-start = ((), (), s32[]{:S(2)}) async-start(), calls=%async_computation.12 | async-start | bytes 294912
  402.1 209.9 %all-reduce.4.cloned.1.call-start = ((), (), s32[]{:S(2)}) async-start(), calls=%async_computation.13 | async-start | bytes 3145728 | tf_op jit(solution)/shard_map/psum | solution.py:219
  552.0 68.2 %copy-start.32 = (f32[7,128]{1,0:T(8,128)}, f32[7,128]{1,0:T(8,128)S(1)}, u32[]{:S(2)}) copy-start(f32[7,128]{1,0:T(8,128)S(1)} %convert_element_type.218) | copy-start | bytes 10756
  612.0 4.4 copy-start.18
  (6 other events, 9.2 us)
Sparse Core Ops, SparseCore 0:
  9.9 48.2 all-gather.3
  60.1 27.8 all-gather.5
  90.0 36.7 all-gather.7
  302.9 62.3 reduce-scatter.15
  368.8 41.2 reduce-scatter.11
  413.3 51.3 reduce-scatter.13
  468.5 33.5 reduce-scatter.17
  505.2 33.6 reduce-scatter.19
  542.1 69.8 all-reduce.3
where the time goes:
time: 633 us; the launch traced here: 627 us
  matrix products  225 us (36%)
  waiting for transfers between devices  207 us (33%)
  local copies, waits for them, and re-layouts  97.9 us (15%)
  other arithmetic  44.5 us (7%)
  blocking collectives  29.5 us (5%)
  between operations  14.8 us (2%)
  starting transfers between devices  7.35 us (1%)
    unnamed x12, waiting for transfers between devices  70 us
    unnamed x110, local copies, waits for them, and re-layouts  63.4 us
    psum x1, waiting for transfers between devices, local(): lax.psum(grad_parts[0].astype(jnp.bfloat16), 'pipe').astype(jnp.float32)  59.5 us
    reduce_scatter x1, waiting for transfers between devices, local(): lax.psum_scatter(grad_terms[2].astype(jnp.bfloat16), 'dp', scatter_dimens...  54.6 us
    dot_general x24, matrix products, masked_scores(): jnp.einsum('qd,kd->qk', queries, key_rows, preferred_element_type=jnp.flo...  41.7 us
    dot_general x16, matrix products, head_forward(): mixed_rows = jnp.dot(weights, values, preferred_element_type=jnp.float32)  37.3 us
    all_gather x1, waiting for transfers between devices, local(): lax.all_gather(qkv_weight, 'dp', axis=1, tiled=True)  21.4 us
    dot_general x2, matrix products, layer_forward(): jnp.einsum('td,sde->ste', normed, qkv_w, preferred_element_type=jnp.float32)  19.1 us
  transfers between devices with their start and end apart: 11, of which 6 were waited for; matrix products, arithmetic and copies ran while one was open for 31% of the time, Pallas kernels for 0%

commit v1 on v0

v1 whole, which is shorter than its diff:
```python
import functools

import jax
import jax.numpy as jnp
from jax import lax
from jax.experimental import pallas as pl
from jax.experimental.pallas import tpu as pltpu
from jax.sharding import PartitionSpec as P

HEADS = 8
HEAD = 128
EPSILON = 1e-05
SCALE = HEAD ** (-0.5)
LOG2E = 1.4426950408889634
GELU_C = 0.7978845608028654
GELU_A = 0.044715
GROUPS = 2
VMEM_LIMIT = 56 * 2**20
PARAM_ROWS = 16

F32 = jnp.float32
BF16 = jnp.bfloat16
ANY = pl.BlockSpec(memory_space=pl.ANY)
VMEM = pl.BlockSpec(memory_space=pltpu.VMEM)


def sds(shape, dtype=BF16):
    return jax.ShapeDtypeStruct(shape, dtype)


def dot_nn(a, b):
    return jnp.dot(a, b, preferred_element_type=F32)


def dot_nt(a, b):
    return lax.dot_general(a, b, (((1,), (1,)), ((), ())), preferred_element_type=F32)


def dot_tn(a, b):
    return lax.dot_general(a, b, (((0,), (0,)), ((), ())), preferred_element_type=F32)


class Mover:
    def __init__(self, sems):
        self.sems = sems
        self.used = 0
        self.open = []

    def start(self, source, target):
        copy = pltpu.make_async_copy(source, target, self.sems.at[self.used])
        self.used += 1
        copy.start()
        return copy

    def put(self, source, target):
        self.open.append(self.start(source, target))

    def finish(self):
        for copy in self.open:
            copy.wait()


def load_rows(move, pieces, target, columns=None):
    source_of = (lambda ref: ref) if columns is None else (lambda ref: ref.at[:, columns])
    if len(pieces) == 1:
        return [move.start(source_of(pieces[0]), target)]
    mine = lax.axis_index("dp")
    rows = pieces[0].shape[0] // 4
    copies = []
    for step in range(4):
        for side in range(2):
            owner = mine ^ (2 * step + side)
            source = pieces[side].at[pl.ds(step * rows, rows)]
            if columns is not None:
                source = pieces[side].at[pl.ds(step * rows, rows), columns]
            copies.append(
                move.start(source, target.at[pl.ds(pl.multiple_of(owner * rows, rows), rows)])
            )
    return copies


def store_rows(move, source, pieces, columns=None):
    if len(pieces) == 1:
        target = pieces[0] if columns is None else pieces[0].at[:, columns]
        move.put(source, target)
        return
    mine = lax.axis_index("dp")
    rows = pieces[0].shape[0] // 4
    for step in range(4):
        for side in (1, 0):
            owner = mine ^ (2 * step + side)
            target = pieces[side].at[pl.ds(step * rows, rows)]
            if columns is not None:
                target = pieces[side].at[pl.ds(step * rows, rows), columns]
            move.put(source.at[pl.ds(pl.multiple_of(owner * rows, rows), rows)], target)


def wait_all(copies):
    for copy in copies:
        copy.wait()


def tiles_of(count, size):
    return [pl.ds(start, min(size, count - start)) for start in range(0, count, size)]


def normal_rows(rows):
    centred = rows - jnp.mean(rows, axis=-1, keepdims=True)
    root = lax.rsqrt(jnp.mean(centred * centred, axis=-1, keepdims=True) + EPSILON)
    return centred * root, root


def column_sum(rows):
    return jnp.sum(rows, axis=0, keepdims=True)


def kernel_call(body, name, inputs, in_specs, outs, scratch, copies, flops):
    moved = sum(a.size * a.dtype.itemsize for a in inputs)
    moved += sum(int(jnp.dtype(o.dtype).itemsize) * functools.reduce(int.__mul__, o.shape) for o in outs)
    return pl.pallas_call(
        body,
        name=name,
        out_shape=outs,
        in_specs=in_specs,
        out_specs=[ANY] * len(outs),
        scratch_shapes=list(scratch) + [pltpu.SemaphoreType.DMA((copies,))],
        compiler_params=pltpu.CompilerParams(vmem_limit_bytes=VMEM_LIMIT),
        cost_estimate=pl.CostEstimate(flops=int(flops), bytes_accessed=int(moved), transcendentals=0),
    )(*inputs)


def ln_both(first, second, params):
    count, width = first.shape

    def body(a_ref, b_ref, p_ref, na_ref, nb_ref, a, b, na, nb, sems):
        move = Mover(sems)
        loads = [move.start(a_ref, a), move.start(b_ref, b)]
        gain = p_ref[0:1, :].astype(F32)
        shift = p_ref[2:3, :].astype(F32)
        for load, rows, held, out in ((loads[0], a, na, na_ref), (loads[1], b, nb, nb_ref)):
            load.wait()
            for part in tiles_of(count, 208):
                z, _ = normal_rows(rows[part, :].astype(F32))
                held[part, :] = (z * gain + shift).astype(BF16)
            move.put(held, out)
        move.finish()

    buf = pltpu.VMEM((count, width), BF16)
    return kernel_call(
        body, "ln_both", (first, second, params), [ANY, ANY, VMEM],
        [sds((count, width))] * 2, [buf] * 4, 4, 8 * 2 * count * width,
    )


def attention_group(normed, weight, params, ids_col, ids_row, group, keep):
    count, width = normed.shape
    heads = HEADS // GROUPS
    side = heads * HEAD
    pieces = len(weight)
    tile = count // 2

    def body(*refs):
        n_ref = refs[0]
        w_refs = refs[1 : 1 + pieces]
        p_ref, col_ref, row_ref = refs[1 + pieces : 4 + pieces]
        rest = refs[4 + pieces :]
        if keep:
            q_out, k_out, v_out, o_out, e_out, l_out = rest[:6]
            normed_v, w_v, q, k, v, o, e_all, inv, sems = rest[6:]
        else:
            o_out = rest[0]
            normed_v, w_v, q, k, v, o, sems = rest[1:]
        move = Mover(sems)
        loads = [move.start(n_ref, normed_v)] + load_rows(move, w_refs, w_v)
        at = group * side
        q_shift = p_ref[3:4, at : at + side].astype(F32)
        v_shift = p_ref[4:5, at : at + side].astype(F32)
        wait_all(loads)
        for part in tiles_of(count, tile):
            projected = dot_nn(normed_v[part, :], w_v[...])
            q[part, :] = (projected[:, :side] + q_shift).astype(BF16)
            k[part, :] = projected[:, side : 2 * side].astype(BF16)
            v[part, :] = (projected[:, 2 * side :] + v_shift).astype(BF16)
        if keep:
            move.put(q, q_out)
            move.put(k, k_out)
            move.put(v, v_out)
        for head in range(heads):
            lanes = pl.ds(head * HEAD, HEAD)
            key_rows = k[:, lanes]
            value_rows = v[:, lanes]
            wide = jnp.concatenate([value_rows, jnp.ones_like(value_rows)], axis=1)
            for part in tiles_of(count, tile):
                scores = dot_nt(q[part, lanes], key_rows)
                scores = jnp.where(col_ref[part, 0:1] == row_ref[...], scores, -1e30)
                top = jnp.max(scores, axis=1, keepdims=True)
                e = jnp.exp2(scores * (SCALE * LOG2E) - top * (SCALE * LOG2E)).astype(BF16)
                if keep:
                    e_all[head, part, :] = e
                both = dot_nn(e, wide)
                inverse = 1.0 / both[:, HEAD:]
                if keep:
                    inv[part, lanes] = inverse
                o[part, lanes] = (both[:, :HEAD] * inverse).astype(BF16)
            if keep:
                move.put(e_all.at[head], e_out.at[head])
        move.put(o, o_out)
        if keep:
            move.put(inv, l_out)
        move.finish()

    buf = pltpu.VMEM((count, side), BF16)
    scratch = [
        pltpu.VMEM((count, width), BF16),
        pltpu.VMEM((width, 3 * side), BF16),
        buf, buf, buf, buf,
    ]
    outs = [sds((count, side))]
    if keep:
        scratch += [pltpu.VMEM((heads, count, count), BF16), pltpu.VMEM((count, side), F32)]
        outs = [sds((count, side))] * 4 + [sds((heads, count, count)), sds((count, side), F32)]
    flops = 2 * count * width * 3 * side + 8 * heads * count * count * HEAD
    return kernel_call(
        body, f"attention_{'stash' if keep else 'fwd'}_{group}",
        (normed, *weight, params, ids_col, ids_row),
        [ANY] * (1 + pieces) + [VMEM] * 3, outs, scratch, 9 + heads + 7, flops,
    )


def gelu_parts(hidden):
    square = hidden * hidden
    bend = jnp.tanh(GELU_C * hidden * (1.0 + GELU_A * square))
    half = 0.5 * (1.0 + bend)
    slope = half + 0.5 * hidden * (1.0 - bend * bend) * (GELU_C * (1.0 + 3.0 * GELU_A * square))
    return hidden * half, slope


def mlp_stash(latents, mixed, weight, params):
    count, width = latents.shape
    pieces = len(weight)
    split = len(mixed)
    tile = count // 4

    def body(*refs):
        x_ref = refs[0]
        m_refs = refs[1 : 1 + split]
        w_refs = refs[1 + split : 1 + split + pieces]
        p_ref = refs[1 + split + pieces]
        n_out, z_out, r_out, a_out, s_out = refs[2 + split + pieces : 7 + split + pieces]
        x, mixed_v, w, n, z_v, r_v, act, slope_v, sems = refs[7 + split + pieces :]
        move = Mover(sems)
        side = width // split
        loads = [move.start(x_ref, x)]
        for index, ref in enumerate(m_refs):
            loads.append(move.start(ref, mixed_v.at[:, pl.ds(index * side, side)]))
        loads += load_rows(move, w_refs, w)
        rows = [p_ref[i : i + 1, :].astype(F32) for i in range(9)]
        wait_all(loads)
        for part in tiles_of(count, tile):
            attended = x[part, :].astype(F32) + dot_nn(mixed_v[part, :], w[:, :width]) + rows[5]
            z, root = normal_rows(attended)
            z_v[part, :] = z.astype(BF16)
            r_v[part, :] = jnp.broadcast_to(root, (tile, 128))
            n[part, :] = (z * rows[1] + rows[6]).astype(BF16)
            hidden = dot_nn(n[part, :], w[:, width:]) + rows[7]
            active, slope = gelu_parts(hidden)
            act[part, :] = active.astype(BF16)
            slope_v[part, :] = slope.astype(BF16)
            for held, out in ((n, n_out), (z_v, z_out), (r_v, r_out), (act, a_out), (slope_v, s_out)):
                move.put(held.at[part], out.at[part])
        move.finish()

    buf = pltpu.VMEM((count, width), BF16)
    return kernel_call(
        body, "mlp_stash", (latents, *mixed, *weight, params),
        [ANY] * (1 + split + pieces) + [VMEM],
        [sds((count, width)), sds((count, width)), sds((count, 128), F32), sds((count, width)), sds((count, width))],
        [buf, buf, pltpu.VMEM((width, 2 * width), BF16), buf, buf, pltpu.VMEM((count, 128), F32), buf, buf],
        1 + split + 8 + 20, 4 * count * width * width,
    )


def mlp_fwd(latents, mixed, weight, last, params, ids_col):
    count, width = latents.shape
    pieces = len(weight)
    split = len(mixed)
    tile = count // 4

    def body(*refs):
        x_ref = refs[0]
        m_refs = refs[1 : 1 + split]
        w_refs = refs[1 + split : 1 + split + pieces]
        l_refs = refs[1 + split + pieces : 1 + split + 2 * pieces]
        p_ref, col_ref, y_out = refs[1 + split + 2 * pieces : 4 + split + 2 * pieces]
        x, mixed_v, w, w_last, y, sems = refs[4 + split + 2 * pieces :]
        move = Mover(sems)
        side = width // split
        loads = [move.start(x_ref, x)]
        for index, ref in enumerate(m_refs):
            loads.append(move.start(ref, mixed_v.at[:, pl.ds(index * side, side)]))
        loads += load_rows(move, w_refs, w)
        loads += load_rows(move, l_refs, w_last)
        rows = [p_ref[i : i + 1, :].astype(F32) for i in range(9)]
        wait_all(loads)
        for part in tiles_of(count, tile):
            attended = x[part, :].astype(F32) + dot_nn(mixed_v[part, :], w[:, :width]) + rows[5]
            z, _ = normal_rows(attended)
            normed = (z * rows[1] + rows[6]).astype(BF16)
            hidden = dot_nn(normed, w[:, width:]) + rows[7]
            active = gelu_parts(hidden)[0].astype(BF16)
            result = attended + dot_nn(active, w_last[...]) + rows[8]
            y[part, :] = jnp.where(col_ref[part, 0:1] < 3, result, 0.0).astype(BF16)
            move.put(y.at[part], y_out.at[part])
        move.finish()

    buf = pltpu.VMEM((count, width), BF16)
    return kernel_call(
        body, "mlp_fwd", (latents, *mixed, *weight, *last, params, ids_col),
        [ANY] * (1 + split + 2 * pieces) + [VMEM] * 2,
        [sds((count, width))],
        [buf, buf, pltpu.VMEM((width, 2 * width), BF16), pltpu.VMEM((width, width), BF16), buf],
        1 + split + 16 + 4, 6 * count * width * width,
    )[0]


def mlp_backward(arrived, ids_col, active, slope, normed, last, shards):
    count, width = active.shape
    pieces = len(last)
    tile = count // 2

    def body(*refs):
        g_ref, a_ref, s_ref, n_ref = refs[:4]
        w_refs = refs[4 : 4 + pieces]
        col_ref = refs[4 + pieces]
        rest = refs[5 + pieces :]
        d_out, c_out, b_out = rest[:3]
        grads = rest[3 : 3 + pieces]
        g, act, slo, n, w, dout, dhid, terms, sums, sems = rest[3 + pieces :]
        move = Mover(sems)
        load_g = move.start(g_ref, g)
        load_w = load_rows(move, w_refs, w)
        load_s = move.start(s_ref, slo)
        load_a = move.start(a_ref, act)
        load_n = move.start(n_ref, n)
        load_g.wait()
        dout[...] = jnp.where(col_ref[:, 0:1] < 3, g[...].astype(F32), 0.0).astype(BF16)
        move.put(dout, c_out)
        wait_all(load_w)
        load_s.wait()
        first = jnp.zeros((1, width), F32)
        second = jnp.zeros((1, width), F32)
        for part in tiles_of(count, tile):
            dactive = dot_nt(dout[part, :], w[...])
            held = (slo[part, :].astype(F32) * dactive).astype(BF16)
            dhid[part, :] = held
            first += column_sum(held.astype(F32))
            second += column_sum(dout[part, :].astype(F32))
        sums[0:1, :] = first
        sums[1:2, :] = second
        move.put(dhid, d_out)
        move.put(sums, b_out)
        load_n.wait()
        terms[:, :width] = dot_tn(n[...], dhid[...]).astype(BF16)
        load_a.wait()
        terms[:, width:] = dot_tn(act[...], dout[...]).astype(BF16)
        store_rows(move, terms, grads)
        move.finish()

    buf = pltpu.VMEM((count, width), BF16)
    return kernel_call(
        body, "mlp_backward", (arrived, active, slope, normed, *last, ids_col),
        [ANY] * (4 + pieces) + [VMEM],
        [sds((count, width)), sds((count, width)), sds((8, width), F32)]
        + [sds((shards, 2 * width))] * pieces,
        [buf, buf, buf, buf, pltpu.VMEM((width, width), BF16), buf, buf,
         pltpu.VMEM((width, 2 * width), BF16), pltpu.VMEM((8, width), F32)],
        4 + 8 + 3 + 8, 6 * count * width * width,
    )


def out_backward(dhidden, dout, z2, root2, mixed, weight, params, shards):
    count, width = dhidden.shape
    pieces = len(weight)
    split = len(mixed)
    tile = count // 4

    def body(*refs):
        h_ref, c_ref, z_ref, r_ref = refs[:4]
        m_refs = refs[4 : 4 + split]
        w_refs = refs[4 + split : 4 + split + pieces]
        p_ref = refs[4 + split + pieces]
        rest = refs[5 + split + pieces :]
        d_out, m_out, b_out = rest[:3]
        grads = rest[3 : 3 + pieces]
        dhid, cot, z_v, r_v, mixed_v, w, datt, dattn, dmix, terms, sums, sems = rest[3 + pieces :]
        move = Mover(sems)
        side = width // split
        loads = [move.start(h_ref, dhid)]
        loads += load_rows(move, w_refs, w)
        loads += [move.start(c_ref, cot), move.start(z_ref, z_v), move.start(r_ref, r_v)]
        late = []
        for index, ref in enumerate(m_refs):
            late.append(move.start(ref, mixed_v.at[:, pl.ds(index * side, side)]))
        gain = p_ref[1:2, :].astype(F32)
        wait_all(loads)
        totals = [jnp.zeros((1, width), F32) for _ in range(3)]
        for part in tiles_of(count, tile):
            dnormed = dot_nt(dhid[part, :], w[:, width:])
            z = z_v[part, :].astype(F32)
            totals[0] += column_sum(dnormed * z)
            totals[1] += column_sum(dnormed)
            dz = dnormed * gain
            inner = dz - jnp.mean(dz, axis=-1, keepdims=True)
            inner = inner - z * jnp.mean(dz * z, axis=-1, keepdims=True)
            dattended = cot[part, :].astype(F32) + r_v[part, 0:1] * inner
            datt[part, :] = dattended
            held = dattended.astype(BF16)
            dattn[part, :] = held
            totals[2] += column_sum(held.astype(F32))
            dmix[part, :] = dot_nt(held, w[:, :width]).astype(BF16)
            move.put(datt.at[part], d_out.at[part])
            move.put(dmix.at[part], m_out.at[part])
        for index in range(3):
            sums[index : index + 1, :] = totals[index]
        move.put(sums, b_out)
        wait_all(late)
        terms[...] = dot_tn(mixed_v[...], dattn[...]).astype(BF16)
        store_rows(move, terms, grads)
        move.finish()

    buf = pltpu.VMEM((count, width), BF16)
    return kernel_call(
        body, "out_backward", (dhidden, dout, z2, root2, *mixed, *weight, params),
        [ANY] * (4 + split + pieces) + [VMEM],
        [sds((count, width), F32), sds((count, width)), sds((8, width), F32)]
        + [sds((shards, width))] * pieces,
        [buf, buf, buf, pltpu.VMEM((count, 128), F32), buf, pltpu.VMEM((width, 2 * width), BF16),
         pltpu.VMEM((count, width), F32), buf, buf, pltpu.VMEM((width, width), BF16),
         pltpu.VMEM((8, width), F32)],
        4 + split + 8 + 8 + 1 + 8, 6 * count * width * width,
    )


def attention_backward(saved, dmixed, normed, group, shards, pieces):
    queries, key_rows, values, mixed, weights, inverse = saved
    count, width = normed.shape
    heads = HEADS // GROUPS
    side = heads * HEAD
    tile = count // 2

    def body(*refs):
        q_ref, k_ref, v_ref, o_ref, e_ref, l_ref, m_ref, n_ref = refs[:8]
        d_out, b_out = refs[8:10]
        grads = refs[10 : 10 + pieces]
        q, k, v, o, e, inv, dmix, n, dqkv, dscore, terms, sums, sems = refs[10 + pieces :]
        move = Mover(sems)
        loads = [
            move.start(m_ref.at[:, pl.ds(group * side, side)], dmix),
            move.start(l_ref, inv), move.start(o_ref, o), move.start(v_ref, v),
            move.start(k_ref, k), move.start(q_ref, q),
        ]
        load_e = [move.start(e_ref.at[head], e.at[head]) for head in range(heads)]
        load_n = move.start(n_ref, n)
        wait_all(loads)
        for head in range(heads):
            lanes = pl.ds(head * HEAD, HEAD)
            scaled = (dmix[:, lanes].astype(F32) * inv[:, lanes]).astype(BF16)
            row_sum = jnp.sum(scaled.astype(F32) * o[:, lanes].astype(F32), axis=1, keepdims=True)
            value_rows = v[:, lanes]
            head_keys = k[:, lanes]
            load_e[head].wait()
            for start in range(0, count, tile):
                part = pl.ds(start, tile)
                dprobs = dot_nt(scaled[start : start + tile], value_rows)
                held = e[head, part, :].astype(F32) * (dprobs - row_sum[start : start + tile])
                held = held.astype(BF16)
                dscore[part, :] = held
                dqkv[part, lanes] = (dot_nn(held, head_keys) * SCALE).astype(BF16)
            dqkv[:, pl.ds(side + head * HEAD, HEAD)] = (
                dot_tn(dscore[...], q[:, lanes]) * SCALE
            ).astype(BF16)
            dqkv[:, pl.ds(2 * side + head * HEAD, HEAD)] = dot_tn(e[head], scaled).astype(BF16)
        move.put(dqkv, d_out)
        sums[0:1, :] = column_sum(dqkv[:, :side].astype(F32))
        sums[1:2, :] = column_sum(dqkv[:, 2 * side :].astype(F32))
        move.put(sums, b_out)
        load_n.wait()
        terms[...] = dot_tn(n[...], dqkv[...]).astype(BF16)
        store_rows(move, terms, grads)
        move.finish()

    buf = pltpu.VMEM((count, side), BF16)
    return kernel_call(
        body, f"attention_backward_{group}",
        (queries, key_rows, values, mixed, weights, inverse, dmixed, normed),
        [ANY] * 8,
        [sds((count, 3 * side)), sds((8, side), F32)] + [sds((shards, 3 * side))] * pieces,
        [buf, buf, buf, buf, pltpu.VMEM((heads, count, count), BF16), pltpu.VMEM((count, side), F32),
         buf, pltpu.VMEM((count, width), BF16), pltpu.VMEM((count, 3 * side), BF16),
         pltpu.VMEM((count, count), BF16), pltpu.VMEM((width, 3 * side), BF16), pltpu.VMEM((8, side), F32)],
        8 + heads + 2 + 8, 2 * count * width * 3 * side + 16 * heads * count * count * HEAD,
    )


def input_backward(latents, dattended, parts, weights, params):
    count, width = latents.shape
    pieces = len(weights[0])
    groups = len(parts)
    side3 = parts[0].shape[1]
    tile = count // 4

    def body(*refs):
        x_ref, d_ref = refs[:2]
        g_refs = refs[2 : 2 + groups]
        at = 2 + groups
        w_refs = [refs[at + i * pieces : at + (i + 1) * pieces] for i in range(groups)]
        at += groups * pieces
        p_ref, y_out, b_out = refs[at : at + 3]
        x, datt, dqkv, w, y, sums, sems = refs[at + 3 :]
        move = Mover(sems)
        loads = []
        for index in range(groups):
            loads.append(move.start(g_refs[index], dqkv.at[index]))
            loads += load_rows(move, w_refs[index], w.at[index])
        loads += [move.start(x_ref, x), move.start(d_ref, datt)]
        gain = p_ref[0:1, :].astype(F32)
        wait_all(loads)
        totals = [jnp.zeros((1, width), F32) for _ in range(2)]
        for part in tiles_of(count, tile):
            dnormed = dot_nt(dqkv[0, part, :], w[0])
            for index in range(1, groups):
                dnormed += dot_nt(dqkv[index, part, :], w[index])
            z, root = normal_rows(x[part, :].astype(F32))
            totals[0] += column_sum(dnormed * z)
            totals[1] += column_sum(dnormed)
            dz = dnormed * gain
            inner = dz - jnp.mean(dz, axis=-1, keepdims=True)
            inner = inner - z * jnp.mean(dz * z, axis=-1, keepdims=True)
            y[part, :] = (datt[part, :] + root * inner).astype(BF16)
            move.put(y.at[part], y_out.at[part])
        for index in range(2):
            sums[index : index + 1, :] = totals[index]
        move.put(sums, b_out)
        move.finish()

    buf = pltpu.VMEM((count, width), BF16)
    return kernel_call(
        body, "input_backward",
        (latents, dattended, *parts, *[piece for weight in weights for piece in weight], params),
        [ANY] * (2 + groups + groups * pieces) + [VMEM],
        [sds((count, width)), sds((8, width), F32)],
        [buf, pltpu.VMEM((count, width), F32), pltpu.VMEM((groups, count, side3), BF16),
         pltpu.VMEM((groups, width, side3), BF16), buf, pltpu.VMEM((8, width), F32)],
        2 + 9 * groups + 5, 2 * count * width * side3 * groups,
    )


def swapped(value, axis, flip):
    count = lax.axis_size(axis)
    return lax.ppermute(value, axis, [(source, source ^ flip) for source in range(count)])


def shifted(value, axis, steps):
    count = lax.axis_size(axis)
    pairs = [(source, (source + steps) % count) for source in range(count)]
    return lax.ppermute(value, axis, pairs)


def after(value, *others):
    return lax.optimization_barrier((value, *others))[0]


def gather_rows(shard):
    if lax.axis_size("dp") != 8:
        return (lax.all_gather(shard, "dp", axis=0, tiled=True),), ()
    arrived = [swapped(shard, "dp", flip) for flip in (2, 4, 6)]
    side = jnp.concatenate([shard, *arrived], axis=0)
    return (side, swapped(side, "dp", 1)), tuple(arrived)


def scatter_sum(pieces):
    if lax.axis_size("dp") != 8:
        return lax.psum_scatter(pieces[0], "dp", scatter_dimension=0, tiled=True)
    mine, theirs = pieces
    other = swapped(theirs, "dp", 1)
    rows = mine.shape[0] // 4
    pair = []
    for step in range(4):
        part = slice(step * rows, (step + 1) * rows)
        pair.append((mine[part].astype(F32) + other[part].astype(F32)).astype(BF16))
    arrived = [swapped(pair[step], "dp", 2 * step) for step in (1, 2, 3)]
    total = pair[0].astype(F32)
    for value in arrived:
        total = total + value.astype(F32)
    return total.astype(BF16)


def pipe_sum(shard):
    count = lax.axis_size("pipe")
    rows = shard.shape[0] // count
    if count != 4 or rows % 16:
        return lax.psum(shard, "pipe")
    place = lax.axis_index("pipe")

    def quarter(step):
        return lax.dynamic_slice_in_dim(shard, (place + step) % count * rows, rows, axis=0)

    total = quarter(0).astype(F32)
    for value in [shifted(quarter(step), "pipe", step) for step in range(1, count)]:
        total = total + value.astype(F32)
    total = total.astype(BF16)
    result = lax.dynamic_update_slice_in_dim(jnp.zeros_like(shard), total, place * rows, axis=0)
    for step, value in [(step, shifted(total, "pipe", step)) for step in range(1, count)]:
        result = lax.dynamic_update_slice_in_dim(
            result, value, (place + count - step) % count * rows, axis=0
        )
    return result


def ordered_sum(value):
    count = lax.axis_size("pipe")
    place = lax.axis_index("pipe")
    blocks = jnp.zeros((count, *value.shape), value.dtype)
    for step in range(count):
        block = shifted(value, "pipe", step) if step else value
        blocks = lax.dynamic_update_index_in_dim(blocks, block, (place + count - step) % count, axis=0)
    total = blocks[0].astype(F32)
    for index in range(1, count):
        total = total + blocks[index].astype(F32)
    return total


def shard_major(rows):
    count = lax.axis_size("dp")
    blocks = rows.reshape(rows.shape[0], count, rows.shape[1] // count).transpose(1, 0, 2)
    if count != 8:
        return (blocks.reshape(-1, blocks.shape[2]),)
    mine = lax.axis_index("dp")

    def pick(flip):
        return lax.dynamic_index_in_dim(blocks, mine ^ flip, axis=0, keepdims=False)

    return tuple(
        jnp.concatenate([pick(2 * step + side) for step in range(4)], axis=0) for side in range(2)
    )


def gather_params(norm_gain, biases):
    width = norm_gain.shape[1]
    count = lax.axis_size("dp")
    shard = jnp.concatenate(
        [norm_gain, biases, jnp.zeros((PARAM_ROWS - 9, width), norm_gain.dtype)], axis=0
    )
    pieces, arrived = gather_rows(shard)
    if len(pieces) == 1:
        blocks = pieces[0].reshape(count, PARAM_ROWS, width)
        return blocks.transpose(1, 0, 2).reshape(PARAM_ROWS, count * width), arrived

    def body(a_ref, b_ref, out):
        mine = lax.axis_index("dp")
        for step in range(4):
            for side, ref in enumerate((a_ref, b_ref)):
                owner = mine ^ (2 * step + side)
                lanes = pl.ds(pl.multiple_of(owner * width, width), width)
                out[:, lanes] = ref[pl.ds(step * PARAM_ROWS, PARAM_ROWS), :]

    full = pl.pallas_call(
        body, name="params_in_order", out_shape=sds((PARAM_ROWS, count * width)),
        in_specs=[VMEM, VMEM], out_specs=VMEM,
    )(*pieces)
    return full, arrived


def local(
    fwd_latents,
    fwd_segments,
    stash_latents,
    stash_segments,
    upstream_grad,
    qkv_weight,
    out_weight,
    mlp_weight,
    norm_gain,
    biases,
):
    fwd_x, stash_x = fwd_latents[0], stash_latents[0]
    count, width = fwd_x.shape
    rows = qkv_weight.shape[1]
    side = width // GROUPS
    pieces = 2 if lax.axis_size("dp") == 8 else 1
    shards = width // pieces
    params, hold = gather_params(norm_gain, biases)
    fwd_row, stash_row = fwd_segments, stash_segments
    fwd_col = jnp.broadcast_to(fwd_segments[0][:, None], (count, 128))
    stash_col = jnp.broadcast_to(stash_segments[0][:, None], (count, 128))
    arrived = shifted(upstream_grad[0], "pipe", -1)

    qkv_parts = []
    for group in range(GROUPS):
        cut = qkv_weight[:, :, group * side : (group + 1) * side]
        shard = jnp.concatenate([cut[0], cut[1], cut[2]], axis=1)
        gathered, hold = gather_rows(after(shard, *hold))
        qkv_parts.append(gathered)
    middle, hold = gather_rows(
        after(jnp.concatenate([out_weight, mlp_weight[0]], axis=1), *hold)
    )
    last, hold = gather_rows(after(mlp_weight[1], *hold))

    fwd_normed, stash_normed = ln_both(fwd_x, stash_x, params)
    saved = []
    fwd_mixed = []
    for group in range(GROUPS):
        saved.append(
            attention_group(stash_normed, qkv_parts[group], params, stash_col, stash_row, group, True)
        )
        fwd_mixed += attention_group(
            fwd_normed, qkv_parts[group], params, fwd_col, fwd_row, group, False
        )
    stash_mixed = [group[3] for group in saved]
    normed2, z2, root2, active, slope = mlp_stash(stash_x, stash_mixed, middle, params)
    result = mlp_fwd(fwd_x, fwd_mixed, middle, last, params, fwd_col)
    latents = shifted(result[None], "pipe", 1)

    dhidden, dout, mlp_sums, *mlp_terms = mlp_backward(
        arrived, stash_col, active, slope, normed2, last, shards
    )
    mlp_total = pipe_sum(scatter_sum(mlp_terms))
    dattended, dmixed, out_sums, *out_terms = out_backward(
        dhidden, dout, z2, root2, stash_mixed, middle, params, shards
    )
    out_total = pipe_sum(scatter_sum(out_terms))
    dprojected, qkv_totals, qkv_sums = [], [], []
    for group in range(GROUPS):
        part, sums, *terms = attention_backward(
            saved[group], dmixed, stash_normed, group, shards, pieces
        )
        dprojected.append(part)
        qkv_sums.append(sums)
        qkv_totals.append(pipe_sum(scatter_sum(terms)))
    input_grad, in_sums = input_backward(stash_x, dattended, dprojected, qkv_parts, params)

    query_shift = jnp.concatenate([sums[0:1] for sums in qkv_sums], axis=1)
    value_shift = jnp.concatenate([sums[1:2] for sums in qkv_sums], axis=1)
    small = jnp.concatenate(
        [
            in_sums[0:1], out_sums[0:1], in_sums[1:2], query_shift, value_shift,
            out_sums[2:3], out_sums[1:2], mlp_sums[0:1], mlp_sums[1:2],
            jnp.zeros((PARAM_ROWS - 9, width), F32),
        ],
        axis=0,
    ).astype(BF16)
    small_sum = ordered_sum(scatter_sum(shard_major(small)))

    qkv_grad = jnp.stack(
        [
            jnp.concatenate([total[:, s * side : (s + 1) * side] for total in qkv_totals], axis=1)
            for s in range(3)
        ]
    ).astype(F32)
    mlp_grad = jnp.stack([mlp_total[:, :width], mlp_total[:, width:]]).astype(F32)
    return (
        latents,
        input_grad[None],
        qkv_grad,
        out_total.astype(F32),
        mlp_grad,
        small_sum[0:2],
        small_sum[2:9],
        small_sum[6],
    )


def solution(mesh):
    in_specs = (
        P("pipe", "dp", None),
        P("pipe", "dp"),
        P("pipe", "dp", None),
        P("pipe", "dp"),
        P("pipe", "dp", None),
        P(None, "dp", None),
        P("dp", None),
        P(None, "dp", None),
        P(None, "dp"),
        P(None, "dp"),
    )
    out_specs = (
        P("pipe", "dp", None),
        P("pipe", "dp", None),
        P(None, "dp", None),
        P("dp", None),
        P(None, "dp", None),
        P(None, "dp"),
        P(None, "dp"),
        P("dp"),
    )
    return jax.shard_map(local, mesh=mesh, in_specs=in_specs, out_specs=out_specs, check_vma=False)
```

time: 633 us -> 459 us (0.73)
  matrix products: 225 us -> 0 us
  Pallas kernels: 0 us -> 163 us
  local copies, waits for them, and re-layouts: 97.9 us -> 16.2 us
  starting transfers between devices: 7.35 us -> 81.5 us
  other arithmetic: 44.5 us -> 8.67 us
  blocking collectives: 29.5 us -> 0 us
  waiting for transfers between devices: 207 us -> 183 us
  between operations: 14.8 us -> 1.86 us
    dot_general x86 -> x0, matrix products: 225 us -> none  [the longest x24 41.7 us: masked_scores(): jnp.einsum('qd,kd->qk', queries, key_rows, preferred_element_type=jnp.flo...]
    pallas_call x0 -> x13, Pallas kernels: none -> 163 us  [the longest x12 161 us: kernel_call(): pl.pallas_call(body, name=name, out_shape=outs, in_specs=in_specs, out_sp...]
    ppermute x0 -> x40, waiting for transfers between devices: none -> 98.6 us  [swapped(): lax.ppermute(value, axis, [(source, source ^ flip) for source in range(co...]
    ppermute x2 -> x29, waiting for transfers between devices: 0.01 us -> 84.7 us  [shifted(): return lax.ppermute(value, axis, pairs)]
    unnamed x12 -> x0, waiting for transfers between devices: 70 us -> none
    psum x1 -> x0, waiting for transfers between devices: 59.5 us -> none  [local(): lax.psum(grad_parts[0].astype(jnp.bfloat16), 'pipe').astype(jnp.float32)]
    reduce_scatter x2 -> x0, waiting for transfers between devices: 56.2 us -> none  [the longest x1 54.6 us: local(): lax.psum_scatter(grad_terms[2].astype(jnp.bfloat16), 'dp', scatter_dimens...]
    unnamed x110 -> x59, local copies, waits for them, and re-layouts: 63.4 us -> 7.67 us
  transfers between devices with their start and end apart: 11 -> 69, of which waited for: 6 -> 32; matrix products, arithmetic and copies ran while one was open for 31% -> 4% of each run, Pallas kernels for 0% -> 19%
where the time goes in v1:
time: 459 us; the launch traced here: 454 us
  waiting for transfers between devices  183 us (40%)
  Pallas kernels  163 us (36%)
  starting transfers between devices  81.5 us (18%)
  local copies, waits for them, and re-layouts  16.2 us (4%)
  other arithmetic  8.67 us (2%)
    pallas_call x12, Pallas kernels, kernel_call(): pl.pallas_call(body, name=name, out_shape=outs, in_specs=in_specs, out_sp...  161 us
    ppermute x40, waiting for transfers between devices, swapped(): lax.ppermute(value, axis, [(source, source ^ flip) for source in range(co...  98.6 us
    ppermute x29, waiting for transfers between devices, shifted(): return lax.ppermute(value, axis, pairs)  84.7 us
    ppermute x29, starting transfers between devices, shifted(): return lax.ppermute(value, axis, pairs)  43.2 us
    ppermute x40, starting transfers between devices, swapped(): lax.ppermute(value, axis, [(source, source ^ flip) for source in range(co...  38.3 us
  transfers between devices with their start and end apart: 69, of which 32 were waited for; matrix products, arithmetic and copies ran while one was open for 4% of the time, Pallas kernels for 19%

profile of v1, /device:TPU:0, one launch (start us, length us, event | category | flops | bytes accessed | tf_op | source)
XLA Modules:
  0.0 454.1 jit_solution(4660662532403037134)
XLA Ops:
  1.4 3.0 collective-permute-start
  8.0 2.4 collective-permute-done.2
  11.0 2.9 collective-permute-start.6
  14.7 7.8 %collective-permute-done.4 = bf16[128,1536]{1,0:T(8,128)(2,1)S(1)} collective-permute-done((bf16[128,1536]{1,0:T(8,128)(2,1)S(1)}, bf16[128,1536]{1,0:T(8,128)(2,1)S(1)}, u32[]{:S(2)}, u32[]{:S(2)}) %collective-permute-start.4) | collective-permute-done | bytes 393248 | tf_op jit(solution)/shard_map/ppermute | solution.py:560
  22.5 5.8 %collective-permute-done.5 = bf16[128,1536]{1,0:T(8,128)(2,1)S(1)} collective-permute-done((bf16[128,1536]{1,0:T(8,128)(2,1)S(1)}, bf16[128,1536]{1,0:T(8,128)(2,1)S(1)}, u32[]{:S(2)}, u32[]{:S(2)}) %collective-permute-start.5) | collective-permute-done | bytes 393248 | tf_op jit(solution)/shard_map/ppermute | solution.py:560
  34.9 5.5 %collective-permute-done.8 = bf16[128,1536]{1,0:T(8,128)(2,1)S(1)} collective-permute-done((bf16[128,1536]{1,0:T(8,128)(2,1)S(1)}, bf16[128,1536]{1,0:T(8,128)(2,1)S(1)}, u32[]{:S(2)}, u32[]{:S(2)}) %collective-permute-start.8) | collective-permute-done | bytes 393248 | tf_op jit(solution)/shard_map/ppermute | solution.py:560
  40.3 5.8 %collective-permute-done.9 = bf16[128,1536]{1,0:T(8,128)(2,1)S(1)} collective-permute-done((bf16[128,1536]{1,0:T(8,128)(2,1)S(1)}, bf16[128,1536]{1,0:T(8,128)(2,1)S(1)}, u32[]{:S(2)}, u32[]{:S(2)}) %collective-permute-start.9) | collective-permute-done | bytes 393248 | tf_op jit(solution)/shard_map/ppermute | solution.py:560
  46.9 2.5 collective-permute-start.13
  51.7 9.7 %collective-permute-done.12 = bf16[128,2048]{1,0:T(8,128)(2,1)S(1)} collective-permute-done((bf16[128,2048]{1,0:T(8,128)(2,1)S(1)}, bf16[128,2048]{1,0:T(8,128)(2,1)S(1)}, u32[]{:S(2)}, u32[]{:S(2)}) %collective-permute-start.12) | collective-permute-done | bytes 524320 | tf_op jit(solution)/shard_map/ppermute | solution.py:560
  61.5 7.0 %collective-permute-done.13 = bf16[128,2048]{1,0:T(8,128)(2,1)S(1)} collective-permute-done((bf16[128,2048]{1,0:T(8,128)(2,1)S(1)}, bf16[128,2048]{1,0:T(8,128)(2,1)S(1)}, u32[]{:S(2)}, u32[]{:S(2)}) %collective-permute-start.13) | collective-permute-done | bytes 524320 | tf_op jit(solution)/shard_map/ppermute | solution.py:560
  70.8 2.1 collective-permute-done.3.b_ref
  75.4 5.8 %ln_both.1 = (bf16[832,1024]{1,0:T(8,128)(2,1)}, bf16[832,1024]{1,0:T(8,128)(2,1)}) custom-call(bf16[832,1024]{1,0:T(8,128)(2,1)} %bitcast.93, bf16[832,1024]{1,0:T(8,128)(2,1)} %bitcast.90, bf16[16,1024]{1,0:T(8,128)(2,1)} %params_in_order.1.p_ref.refs_3_.refs_7_.refs_5_.refs_8_), custom_call_target="tpu_custom_call" | custom-call | flops 13631488 | bytes 6848512 | tf_op jit(solution)/shard_map/ln_both/pallas_call | solution.py:120
  82.4 4.4 collective-permute-start.21
  86.8 3.5 collective-permute-done.18
  91.4 13.8 %attention_stash_0.1 = (bf16[832,512]{1,0:T(8,128)(2,1)}, bf16[832,512]{1,0:T(8,128)(2,1)}, bf16[832,512]{1,0:T(8,128)(2,1)}, bf16[832,512]{1,0:T(8,128)(2,1)}, ...) custom-call(bf16[832,1024]{1,0:T(8,128)(2,1)} %get-tuple-element.56.refs_0_.refs_7_, ...), custom_call_target="tpu_custom_call" | custom-call | flops 5452595200 | bytes 15961344 | tf_op jit(solution)/shard_map/attention_stash_0/pallas_call | solution.py:120
  105.2 14.0 %attention_stash_1.1 = (bf16[832,512]{1,0:T(8,128)(2,1)}, bf16[832,512]{1,0:T(8,128)(2,1)}, bf16[832,512]{1,0:T(8,128)(2,1)}, bf16[832,512]{1,0:T(8,128)(2,1)}, ...) custom-call(bf16[832,1024]{1,0:T(8,128)(2,1)} %get-tuple-element.56.refs_0_.refs_7_, ...), custom_call_target="tpu_custom_call" | custom-call | flops 5452595200 | bytes 15961344 | tf_op jit(solution)/shard_map/attention_stash_1/pallas_call | solution.py:120
  119.2 12.1 %mlp_stash.1 = (bf16[832,1024]{1,0:T(8,128)(2,1)}, bf16[832,1024]{1,0:T(8,128)(2,1)}, f32[832,128]{1,0:T(8,128)}, bf16[832,1024]{1,0:T(8,128)(2,1)}, bf16[832,1024]{1,0:T(8,128)(2,1)}) custom-call(bf16[832,1024]{1,0:T(8,128)(2,1)} %bitcast.91, bf16[832,512]{1,0:T(8,128)(2,1)} %get-tuple-element.57.refs_1_.refs_4_.refs_3_, ...), custom_call_target="tpu_custom_call" | custom-call | flops 3489660928 | bytes 14876672 | tf_op jit(solution)/shard_map/mlp_stash/pallas_call | solution.py:120
  133.0 13.2 %mlp_backward.1 = (bf16[832,1024]{1,0:T(8,128)(2,1)}, bf16[832,1024]{1,0:T(8,128)(2,1)}, f32[8,1024]{1,0:T(8,128)}, bf16[512,2048]{1,0:T(8,128)(2,1)}, bf16[512,2048]{1,0:T(8,128)(2,1)}) custom-call(bf16[832,1024]{1,0:T(8,128)(2,1)} %copy-done.19, bf16[832,1024]{1,0:T(8,128)(2,1)} %get-tuple-element.59.refs_1_, bf16[832,1024]{1,0:T(8,128)(2,1)} %get-tuple-element.60.refs_2_, ...), custom_call_target="tpu_custom_call" | custom-call | flops 5234491392 | bytes 16973824 | tf_op jit(solution)/shard_map/mlp_backward/pallas_call | solution.py:120
  146.2 14.8 %out_backward.1 = (f32[832,1024]{1,0:T(8,128)}, bf16[832,1024]{1,0:T(8,128)(2,1)}, f32[8,1024]{1,0:T(8,128)}, bf16[512,1024]{1,0:T(8,128)(2,1)}, bf16[512,1024]{1,0:T(8,128)(2,1)}) custom-call(bf16[832,1024]{1,0:T(8,128)(2,1)} %get-tuple-element.62.refs_0_, bf16[832,1024]{1,0:T(8,128)(2,1)} %get-tuple-element.63.refs_1_, ...), custom_call_target="tpu_custom_call" | custom-call | flops 5234491392 | bytes 18710528 | tf_op jit(solution)/shard_map/out_backward/pallas_call | solution.py:120
  161.8 16.2 %attention_backward_0.1 = (bf16[832,1536]{1,0:T(8,128)(2,1)}, f32[8,512]{1,0:T(8,128)}, bf16[512,1536]{1,0:T(8,128)(2,1)}, bf16[512,1536]{1,0:T(8,128)(2,1)}) custom-call(bf16[832,512]{1,0:T(8,128)(2,1)} %get-tuple-element.67.refs_0_, bf16[832,512]{1,0:T(8,128)(2,1)} %get-tuple-element.68.refs_1_, bf16[832,512]{1,0:T(8,128)(2,1)} %get-tuple-element.69.refs_2_, ...), custom_call_target="tpu_custom_call" | custom-call | flops 8287944704 | bytes 19775488 | tf_op jit(solution)/shard_map/attention_backward_0/pallas_call | solution.py:120
  178.0 15.9 %attention_backward_1.1 = (bf16[832,1536]{1,0:T(8,128)(2,1)}, f32[8,512]{1,0:T(8,128)}, bf16[512,1536]{1,0:T(8,128)(2,1)}, bf16[512,1536]{1,0:T(8,128)(2,1)}) custom-call(bf16[832,512]{1,0:T(8,128)(2,1)} %get-tuple-element.74.refs_0_, bf16[832,512]{1,0:T(8,128)(2,1)} %get-tuple-element.75.refs_1_, bf16[832,512]{1,0:T(8,128)(2,1)} %get-tuple-element.76.refs_2_, ...), custom_call_target="tpu_custom_call" | custom-call | flops 8287944704 | bytes 19775488 | tf_op jit(solution)/shard_map/attention_backward_1/pallas_call | solution.py:120
  193.9 16.0 %input_backward.1 = (bf16[832,1024]{1,0:T(8,128)(2,1)}, f32[8,1024]{1,0:T(8,128)}) custom-call(bf16[832,1024]{1,0:T(8,128)(2,1)} %bitcast.92, f32[832,1024]{1,0:T(8,128)} %get-tuple-element.66.refs_1_, bf16[832,1536]{1,0:T(8,128)(2,1)} %get-tuple-element.73.refs_2_, bf16[832,1536]{1,0:T(8,128)(2,1)} %get-tuple-element.79.refs_3_, ...), custom_call_target="tpu_custom_call" | custom-call | flops 5234491392 | bytes 18284544 | tf_op jit(solution)/shard_map/input_backward/pallas_call | solution.py:120
  213.5 12.8 %attention_fwd_0.1.refs_1_ = bf16[832,512]{1,0:T(8,128)(2,1)} custom-call(bf16[832,1024]{1,0:T(8,128)(2,1)} %get-tuple-element.51.refs_0_, bf16[512,1536]{1,0:T(8,128)(2,1)} %constant_dynamic-update-slice_fusion.refs_1_.refs_4_, bf16[512,1536]{1,0:T(8,128)(2,1)} %collective-permute-done.7.refs_2_.refs_5_, ...), custom_call_target="tpu_custom_call" | custom-call | flops 5452595200 | bytes 6163712 | tf_op jit(solution)/shard_map/attention_fwd_0/pallas_call | solution.py:120
  229.8 13.2 %attention_fwd_1.1.refs_2_ = bf16[832,512]{1,0:T(8,128)(2,1)} custom-call(bf16[832,1024]{1,0:T(8,128)(2,1)} %get-tuple-element.51.refs_0_, bf16[512,1536]{1,0:T(8,128)(2,1)} %constant_dynamic-update-slice_fusion.4.refs_1_.refs_6_, bf16[512,1536]{1,0:T(8,128)(2,1)} %collective-permute-done.11.refs_2_.refs_7_, ...), custom_call_target="tpu_custom_call" | custom-call | flops 5452595200 | bytes 6163712 | tf_op jit(solution)/shard_map/attention_fwd_1/pallas_call | solution.py:120
  245.0 13.4 %mlp_fwd.1 = bf16[832,1024]{1,0:T(8,128)(2,1)} custom-call(bf16[832,1024]{1,0:T(8,128)(2,1)} %bitcast.94, bf16[832,512]{1,0:T(8,128)(2,1)} %attention_fwd_0.1.refs_1_, bf16[832,512]{1,0:T(8,128)(2,1)} %attention_fwd_1.1.refs_2_, bf16[512,2048]{1,0:T(8,128)(2,1)} %copy-done.6, bf16[512,2048]{1,0:T(8,128)(2,1)} %collective-permute-done.15.refs_4_.refs_7_, ...), custom_call_target="tpu_custom_call" | custom-call | flops 5234491392 | bytes 11862016 | tf_op jit(solution)/shard_map/mlp_fwd/pallas_call | solution.py:120
  258.4 2.7 collective-permute-start.67
  269.2 6.1 %collective-permute-done.45 = bf16[128,1024]{1,0:T(8,128)(2,1)S(1)} collective-permute-done((bf16[128,1024]{1,0:T(8,128)(2,1)S(1)}, bf16[128,1024]{1,0:T(8,128)(2,1)S(1)}, u32[]{:S(2)}, u32[]{:S(2)}) %collective-permute-start.45) | collective-permute-done | bytes 262176 | tf_op jit(solution)/shard_map/ppermute | solution.py:560
  275.3 3.3 collective-permute-done.44
  278.8 3.2 collective-permute-start.48
  286.3 38.8 %collective-permute-done.47 = bf16[32,1024]{1,0:T(8,128)(2,1)S(1)} collective-permute-done((bf16[32,1024]{1,0:T(8,128)(2,1)S(1)}, bf16[32,1024]{1,0:T(8,128)(2,1)S(1)}, u32[]{:S(2)}, u32[]{:S(2)}) %collective-permute-start.47) | collective-permute-done | bytes 65568 | tf_op jit(solution)/shard_map/ppermute | solution.py:566
  325.7 5.8 %collective-permute-done.49 = bf16[32,1024]{1,0:T(8,128)(2,1)S(1)} collective-permute-done((bf16[32,1024]{1,0:T(8,128)(2,1)S(1)}, bf16[32,1024]{1,0:T(8,128)(2,1)S(1)}, u32[]{:S(2)}, u32[]{:S(2)}) %collective-permute-start.49) | collective-permute-done | bytes 65568 | tf_op jit(solution)/shard_map/ppermute | solution.py:566
  331.5 5.4 %collective-permute-done.50 = bf16[32,1024]{1,0:T(8,128)(2,1)S(1)} collective-permute-done((bf16[32,1024]{1,0:T(8,128)(2,1)S(1)}, bf16[32,1024]{1,0:T(8,128)(2,1)S(1)}, u32[]{:S(2)}, u32[]{:S(2)}) %collective-permute-start.50) | collective-permute-done | bytes 65568 | tf_op jit(solution)/shard_map/ppermute | solution.py:566
  337.6 3.6 collective-permute-done.51
  347.8 7.5 %collective-permute-done.35 = bf16[128,1536]{1,0:T(8,128)(2,1)S(1)} collective-permute-done((bf16[128,1536]{1,0:T(8,128)(2,1)S(1)}, bf16[128,1536]{1,0:T(8,128)(2,1)S(1)}, u32[]{:S(2)}, u32[]{:S(2)}) %collective-permute-start.35) | collective-permute-done | bytes 393248 | tf_op jit(solution)/shard_map/ppermute | solution.py:560
  356.6 7.2 %collective-permute-done.34 = bf16[128,1536]{1,0:T(8,128)(2,1)S(1)} collective-permute-done((bf16[128,1536]{1,0:T(8,128)(2,1)S(1)}, bf16[128,1536]{1,0:T(8,128)(2,1)S(1)}, u32[]{:S(2)}, u32[]{:S(2)}) %collective-permute-start.34) | collective-permute-done | bytes 393248 | tf_op jit(solution)/shard_map/ppermute | solution.py:560
  365.3 5.8 %collective-permute-start.38 = (bf16[32,1536]{1,0:T(8,128)(2,1)S(1)}, bf16[32,1536]{1,0:T(8,128)(2,1)S(1)}, u32[]{:S(2)}, u32[]{:S(2)}) collective-permute-start(bf16[32,1536]{1,0:T(8,128)(2,1)S(1)} %get-tuple-element.139), channel_id=1, source_target_pairs={{0,24},{8,0},{16,8},{24,16},{1,25},{9,1},{17,9},{25,17},{2,26},{10... | collective-permute-start | bytes 294920 | tf_op jit(solution)/shard_map/ppermute | solution.py:566
  371.1 5.6 %collective-permute-done.24 = bf16[128,1536]{1,0:T(8,128)(2,1)S(1)} collective-permute-done((bf16[128,1536]{1,0:T(8,128)(2,1)S(1)}, bf16[128,1536]{1,0:T(8,128)(2,1)S(1)}, u32[]{:S(2)}, u32[]{:S(2)}) %collective-permute-start.24) | collective-permute-done | bytes 393248 | tf_op jit(solution)/shard_map/ppermute | solution.py:560
  377.1 3.9 collective-permute-start.28
  381.8 2.4 collective-permute-done.36
  384.6 2.3 collective-permute-start.40
  386.9 8.6 %collective-permute-done.27 = bf16[32,1536]{1,0:T(8,128)(2,1)S(1)} collective-permute-done((bf16[32,1536]{1,0:T(8,128)(2,1)S(1)}, bf16[32,1536]{1,0:T(8,128)(2,1)S(1)}, u32[]{:S(2)}, u32[]{:S(2)}) %collective-permute-start.27) | collective-permute-done | bytes 98336 | tf_op jit(solution)/shard_map/ppermute | solution.py:566
  398.4 2.5 collective-permute-start.31
  406.6 10.2 %collective-permute-done.55 = bf16[128,2048]{1,0:T(8,128)(2,1)S(1)} collective-permute-done((bf16[128,2048]{1,0:T(8,128)(2,1)S(1)}, bf16[128,2048]{1,0:T(8,128)(2,1)S(1)}, u32[]{:S(2)}, u32[]{:S(2)}) %collective-permute-start.55) | collective-permute-done | bytes 524320 | tf_op jit(solution)/shard_map/ppermute | solution.py:560
  416.7 8.1 %collective-permute-done.54 = bf16[128,2048]{1,0:T(8,128)(2,1)S(1)} collective-permute-done((bf16[128,2048]{1,0:T(8,128)(2,1)S(1)}, bf16[128,2048]{1,0:T(8,128)(2,1)S(1)}, u32[]{:S(2)}, u32[]{:S(2)}) %collective-permute-start.54) | collective-permute-done | bytes 524320 | tf_op jit(solution)/shard_map/ppermute | solution.py:560
  428.9 2.4 collective-permute-done.58
  431.3 7.6 %collective-permute-done.57 = bf16[32,2048]{1,0:T(8,128)(2,1)S(1)} collective-permute-done((bf16[32,2048]{1,0:T(8,128)(2,1)S(1)}, bf16[32,2048]{1,0:T(8,128)(2,1)S(1)}, u32[]{:S(2)}, u32[]{:S(2)}) %collective-permute-start.57) | collective-permute-done | bytes 131104 | tf_op jit(solution)/shard_map/ppermute | solution.py:566
  443.3 2.9 collective-permute-start.61
  446.2 5.4 %collective-permute-done.60 = bf16[32,2048]{1,0:T(8,128)(2,1)S(1)} collective-permute-done((bf16[32,2048]{1,0:T(8,128)(2,1)S(1)}, bf16[32,2048]{1,0:T(8,128)(2,1)S(1)}, u32[]{:S(2)}, u32[]{:S(2)}) %collective-permute-start.60) | collective-permute-done | bytes 131104 | tf_op jit(solution)/shard_map/ppermute | solution.py:566
  (241 shorter events, 77.8 us)
Async XLA Ops:
  10.5 12.1 %collective-permute-start.4 = (bf16[128,1536]{1,0:T(8,128)(2,1)S(1)}, bf16[128,1536]{1,0:T(8,128)(2,1)S(1)}, u32[]{:S(2)}, u32[]{:S(2)}) collective-permute-start(bf16[128,1536]{1,0:T(8,128)(2,1)S(1)} %pad_maximum_fusion.1), channel_id=1, source_target_pairs={{0,2},{1,3},{2,0},{3,1},{4,6},{5,7},{6,4},{7,5},{8,10},{9,11},{10,... | collective-permute-start | bytes 1179656 | tf_op jit(solution)/shard_map/ppermute | solution.py:560
  11.0 17.3 %collective-permute-start.5 = (bf16[128,1536]{1,0:T(8,128)(2,1)S(1)}, bf16[128,1536]{1,0:T(8,128)(2,1)S(1)}, u32[]{:S(2)}, u32[]{:S(2)}) collective-permute-start(bf16[128,1536]{1,0:T(8,128)(2,1)S(1)} %pad_maximum_fusion.1), channel_id=1, source_target_pairs={{0,4},{1,5},{2,6},{3,7},{4,0},{5,1},{6,2},{7,3},{8,12},{9,13},{10,... | collective-permute-start | bytes 1179656 | tf_op jit(solution)/shard_map/ppermute | solution.py:560
  11.0 17.2 %collective-permute-start.6 = (bf16[128,1536]{1,0:T(8,128)(2,1)S(1)}, bf16[128,1536]{1,0:T(8,128)(2,1)S(1)}, u32[]{:S(2)}, u32[]{:S(2)}) collective-permute-start(bf16[128,1536]{1,0:T(8,128)(2,1)S(1)} %pad_maximum_fusion.1), channel_id=1, source_target_pairs={{0,6},{1,7},{2,4},{3,5},{4,2},{5,3},{6,0},{7,1},{8,14},{9,15},{10,... | collective-permute-start | bytes 1179656 | tf_op jit(solution)/shard_map/ppermute | solution.py:560
  28.3 12.1 %collective-permute-start.8 = (bf16[128,1536]{1,0:T(8,128)(2,1)S(1)}, bf16[128,1536]{1,0:T(8,128)(2,1)S(1)}, u32[]{:S(2)}, u32[]{:S(2)}) collective-permute-start(bf16[128,1536]{1,0:T(8,128)(2,1)S(1)} %pad_maximum_fusion.2), channel_id=1, source_target_pairs={{0,2},{1,3},{2,0},{3,1},{4,6},{5,7},{6,4},{7,5},{8,10},{9,11},{10,... | collective-permute-start | bytes 1179656 | tf_op jit(solution)/shard_map/ppermute | solution.py:560
  29.9 16.2 %collective-permute-start.9 = (bf16[128,1536]{1,0:T(8,128)(2,1)S(1)}, bf16[128,1536]{1,0:T(8,128)(2,1)S(1)}, u32[]{:S(2)}, u32[]{:S(2)}) collective-permute-start(bf16[128,1536]{1,0:T(8,128)(2,1)S(1)} %pad_maximum_fusion.2), channel_id=1, source_target_pairs={{0,4},{1,5},{2,6},{3,7},{4,0},{5,1},{6,2},{7,3},{8,12},{9,13},{10,... | collective-permute-start | bytes 1179656 | tf_op jit(solution)/shard_map/ppermute | solution.py:560
  30.3 16.3 %collective-permute-start.10 = (bf16[128,1536]{1,0:T(8,128)(2,1)S(1)}, bf16[128,1536]{1,0:T(8,128)(2,1)S(1)}, u32[]{:S(2)}, u32[]{:S(2)}) collective-permute-start(bf16[128,1536]{1,0:T(8,128)(2,1)S(1)} %pad_maximum_fusion.2), channel_id=1, source_target_pairs={{0,6},{1,7},{2,4},{3,5},{4,2},{5,3},{6,0},{7,1},{8,14},{9,15},{10,... | collective-permute-start | bytes 1179656 | tf_op jit(solution)/shard_map/ppermute | solution.py:560
  34.1 56.3 %collective-permute-start.7 = (bf16[512,1536]{1,0:T(8,128)(2,1)}, bf16[512,1536]{1,0:T(8,128)(2,1)}, u32[]{:S(2)}, u32[]{:S(2)}) collective-permute-start(bf16[512,1536]{1,0:T(8,128)(2,1)} %constant_dynamic-update-slice_fusion.refs_1_.refs_4_), channel_id=1, source_target_pairs={{0,1},{1,0},{2,3},{3,2},{4,5},{5,4},{6,7},{7,6},{8,9},{9,8},{10,11... | collective-permute-start | bytes 4718600 | tf_op jit(solution)/shard_map/ppermute | solution.py:560
  46.6 14.9 %collective-permute-start.12 = (bf16[128,2048]{1,0:T(8,128)(2,1)S(1)}, bf16[128,2048]{1,0:T(8,128)(2,1)S(1)}, u32[]{:S(2)}, u32[]{:S(2)}) collective-permute-start(bf16[128,2048]{1,0:T(8,128)(2,1)S(1)} %pad_maximum_fusion), channel_id=1, source_target_pairs={{0,2},{1,3},{2,0},{3,1},{4,6},{5,7},{6,4},{7,5},{8,10},{9,11},{10,... | collective-permute-start | bytes 1572872 | tf_op jit(solution)/shard_map/ppermute | solution.py:560
  46.9 21.6 %collective-permute-start.13 = (bf16[128,2048]{1,0:T(8,128)(2,1)S(1)}, bf16[128,2048]{1,0:T(8,128)(2,1)S(1)}, u32[]{:S(2)}, u32[]{:S(2)}) collective-permute-start(bf16[128,2048]{1,0:T(8,128)(2,1)S(1)} %pad_maximum_fusion), channel_id=1, source_target_pairs={{0,4},{1,5},{2,6},{3,7},{4,0},{5,1},{6,2},{7,3},{8,12},{9,13},{10,... | collective-permute-start | bytes 1572872 | tf_op jit(solution)/shard_map/ppermute | solution.py:560
  49.4 19.1 %collective-permute-start.14 = (bf16[128,2048]{1,0:T(8,128)(2,1)S(1)}, bf16[128,2048]{1,0:T(8,128)(2,1)S(1)}, u32[]{:S(2)}, u32[]{:S(2)}) collective-permute-start(bf16[128,2048]{1,0:T(8,128)(2,1)S(1)} %pad_maximum_fusion), channel_id=1, source_target_pairs={{0,6},{1,7},{2,4},{3,5},{4,2},{5,3},{6,0},{7,1},{8,14},{9,15},{10,... | collective-permute-start | bytes 1572872 | tf_op jit(solution)/shard_map/ppermute | solution.py:560
  68.6 50.6 %collective-permute-start.15 = (bf16[512,2048]{1,0:T(8,128)(2,1)S(1)}, bf16[512,2048]{1,0:T(8,128)(2,1)}, u32[]{:S(2)}, u32[]{:S(2)}) collective-permute-start(bf16[512,2048]{1,0:T(8,128)(2,1)S(1)} %constant_dynamic-update-slice_fusion.8.refs_3_.refs_6_), channel_id=1, source_target_pairs={{0,1},{1,0},{2,3},{3,2},{4,5},{5,4},{6,7},{7,6},{8,9},{9,8},{10,11... | collective-permute-start | bytes 6291464 | tf_op jit(solution)/shard_map/ppermute | solution.py:560
  69.6 35.6 %collective-permute-start.11 = (bf16[512,1536]{1,0:T(8,128)(2,1)}, bf16[512,1536]{1,0:T(8,128)(2,1)}, u32[]{:S(2)}, u32[]{:S(2)}) collective-permute-start(bf16[512,1536]{1,0:T(8,128)(2,1)} %constant_dynamic-update-slice_fusion.4.refs_1_.refs_6_), channel_id=1, source_target_pairs={{0,1},{1,0},{2,3},{3,2},{4,5},{5,4},{6,7},{7,6},{8,9},{9,8},{10,11... | collective-permute-start | bytes 4718600 | tf_op jit(solution)/shard_map/ppermute | solution.py:560
  70.0 11.2 %collective-permute-start.16 = (bf16[128,1024]{1,0:T(8,128)(2,1)S(1)}, bf16[128,1024]{1,0:T(8,128)(2,1)S(1)}, u32[]{:S(2)}, u32[]{:S(2)}) collective-permute-start(bf16[128,1024]{1,0:T(8,128)(2,1)S(1)} %get-tuple-element.55), channel_id=1, source_target_pairs={{0,2},{1,3},{2,0},{3,1},{4,6},{5,7},{6,4},{7,5},{8,10},{9,11},{10,... | collective-permute-start | bytes 786440 | tf_op jit(solution)/shard_map/ppermute | solution.py:560
  82.4 49.0 %collective-permute-start.21 = (bf16[832,1024]{1,0:T(8,128)(2,1)S(1)}, bf16[832,1024]{1,0:T(8,128)(2,1)S(1)}, u32[]{:S(2)}, u32[]{:S(2)}) collective-permute-start(bf16[832,1024]{1,0:T(8,128)(2,1)S(1)} %bitcast.95), channel_id=1, source_target_pairs={{0,24},{8,0},{16,8},{24,16},{1,25},{9,1},{17,9},{25,17},{2,26},{10... | collective-permute-start | bytes 5111816 | tf_op jit(solution)/shard_map/ppermute | solution.py:566
  90.3 41.1 %collective-permute-start.19 = (bf16[512,1024]{1,0:T(8,128)(2,1)S(1)}, bf16[512,1024]{1,0:T(8,128)(2,1)S(1)}, u32[]{:S(2)}, u32[]{:S(2)}) collective-permute-start(bf16[512,1024]{1,0:T(8,128)(2,1)S(1)} %constant_dynamic-update-slice_fusion.12.refs_5_.refs_4_), channel_id=1, source_target_pairs={{0,1},{1,0},{2,3},{3,2},{4,5},{5,4},{6,7},{7,6},{8,9},{9,8},{10,11... | collective-permute-start | bytes 3145736 | tf_op jit(solution)/shard_map/ppermute | solution.py:560
  212.0 14.2 %collective-permute-start.62 = (bf16[64,128]{1,0:T(8,128)(2,1)S(1)}, bf16[64,128]{1,0:T(8,128)(2,1)S(1)}, u32[]{:S(2)}, u32[]{:S(2)}) collective-permute-start(bf16[64,128]{1,0:T(8,128)(2,1)S(1)} %pad_maximum_fusion.3), channel_id=1, source_target_pairs={{0,1},{1,0},{2,3},{3,2},{4,5},{5,4},{6,7},{7,6},{8,9},{9,8},{10,11... | collective-permute-start | bytes 49160 | tf_op jit(solution)/shard_map/ppermute | solution.py:560
  226.3 17.3 %collective-permute-start.65 = (bf16[16,128]{1,0:T(8,128)(2,1)S(1)}, bf16[16,128]{1,0:T(8,128)(2,1)S(1)}, u32[]{:S(2)}, u32[]{:S(2)}) collective-permute-start(bf16[16,128]{1,0:T(8,128)(2,1)S(1)} %get-tuple-element.145), channel_id=1, source_target_pairs={{0,6},{1,7},{2,4},{3,5},{4,2},{5,3},{6,0},{7,1},{8,14},{9,15},{10,... | collective-permute-start | bytes 12296 | tf_op jit(solution)/shard_map/ppermute | solution.py:560
  227.6 16.1 %collective-permute-start.64 = (bf16[16,128]{1,0:T(8,128)(2,1)S(1)}, bf16[16,128]{1,0:T(8,128)(2,1)S(1)}, u32[]{:S(2)}, u32[]{:S(2)}) collective-permute-start(bf16[16,128]{1,0:T(8,128)(2,1)S(1)} %get-tuple-element.146), channel_id=1, source_target_pairs={{0,4},{1,5},{2,6},{3,7},{4,0},{5,1},{6,2},{7,3},{8,12},{9,13},{10,... | collective-permute-start | bytes 12296 | tf_op jit(solution)/shard_map/ppermute | solution.py:560
  228.9 14.7 %collective-permute-start.63 = (bf16[16,128]{1,0:T(8,128)(2,1)S(1)}, bf16[16,128]{1,0:T(8,128)(2,1)S(1)}, u32[]{:S(2)}, u32[]{:S(2)}) collective-permute-start(bf16[16,128]{1,0:T(8,128)(2,1)S(1)} %get-tuple-element.144), channel_id=1, source_target_pairs={{0,2},{1,3},{2,0},{3,1},{4,6},{5,7},{6,4},{7,5},{8,10},{9,11},{10,... | collective-permute-start | bytes 12296 | tf_op jit(solution)/shard_map/ppermute | solution.py:560
  243.0 99.0 %collective-permute-start.32 = (bf16[512,1536]{1,0:T(8,128)(2,1)}, bf16[512,1536]{1,0:T(8,128)(2,1)S(1)}, u32[]{:S(2)}, u32[]{:S(2)}) collective-permute-start(bf16[512,1536]{1,0:T(8,128)(2,1)} %get-tuple-element.84), channel_id=1, source_target_pairs={{0,1},{1,0},{2,3},{3,2},{4,5},{5,4},{6,7},{7,6},{8,9},{9,8},{10,11... | collective-permute-start | bytes 4718600 | tf_op jit(solution)/shard_map/ppermute | solution.py:560
  243.1 102.0 %collective-permute-start.22 = (bf16[512,1536]{1,0:T(8,128)(2,1)S(1)}, bf16[512,1536]{1,0:T(8,128)(2,1)S(1)}, u32[]{:S(2)}, u32[]{:S(2)}) collective-permute-start(bf16[512,1536]{1,0:T(8,128)(2,1)S(1)} %copy-done.20), channel_id=1, source_target_pairs={{0,1},{1,0},{2,3},{3,2},{4,5},{5,4},{6,7},{7,6},{8,9},{9,8},{10,11... | collective-permute-start | bytes 4718600 | tf_op jit(solution)/shard_map/ppermute | solution.py:560
  243.6 21.1 %collective-permute-start.42 = (bf16[512,1024]{1,0:T(8,128)(2,1)S(1)}, bf16[512,1024]{1,0:T(8,128)(2,1)S(1)}, u32[]{:S(2)}, u32[]{:S(2)}) collective-permute-start(bf16[512,1024]{1,0:T(8,128)(2,1)S(1)} %copy-done.22), channel_id=1, source_target_pairs={{0,1},{1,0},{2,3},{3,2},{4,5},{5,4},{6,7},{7,6},{8,9},{9,8},{10,11... | collective-permute-start | bytes 3145736 | tf_op jit(solution)/shard_map/ppermute | solution.py:560
  243.7 17.4 %collective-permute-start.66 = (bf16[16,128]{1,0:T(8,128)(2,1)S(1)}, bf16[16,128]{1,0:T(8,128)(2,1)S(1)}, u32[]{:S(2)}, u32[]{:S(2)}) collective-permute-start(bf16[16,128]{1,0:T(8,128)(2,1)S(1)} %get-tuple-element.95), channel_id=1, source_target_pairs={{0,8},{8,16},{16,24},{24,0},{1,9},{9,17},{17,25},{25,1},{2,10},{10... | collective-permute-start | bytes 12296 | tf_op jit(solution)/shard_map/ppermute | solution.py:566
  265.0 10.2 %collective-permute-start.45 = (bf16[128,1024]{1,0:T(8,128)(2,1)S(1)}, bf16[128,1024]{1,0:T(8,128)(2,1)S(1)}, u32[]{:S(2)}, u32[]{:S(2)}) collective-permute-start(bf16[128,1024]{1,0:T(8,128)(2,1)S(1)} %get-tuple-element.114), channel_id=1, source_target_pairs={{0,6},{1,7},{2,4},{3,5},{4,2},{5,3},{6,0},{7,1},{8,14},{9,15},{10,... | collective-permute-start | bytes 786440 | tf_op jit(solution)/shard_map/ppermute | solution.py:560
  266.7 11.9 %collective-permute-start.44 = (bf16[128,1024]{1,0:T(8,128)(2,1)S(1)}, bf16[128,1024]{1,0:T(8,128)(2,1)S(1)}, u32[]{:S(2)}, u32[]{:S(2)}) collective-permute-start(bf16[128,1024]{1,0:T(8,128)(2,1)S(1)} %get-tuple-element.115), channel_id=1, source_target_pairs={{0,4},{1,5},{2,6},{3,7},{4,0},{5,1},{6,2},{7,3},{8,12},{9,13},{10,... | collective-permute-start | bytes 786440 | tf_op jit(solution)/shard_map/ppermute | solution.py:560
  267.8 10.8 %collective-permute-start.43 = (bf16[128,1024]{1,0:T(8,128)(2,1)S(1)}, bf16[128,1024]{1,0:T(8,128)(2,1)S(1)}, u32[]{:S(2)}, u32[]{:S(2)}) collective-permute-start(bf16[128,1024]{1,0:T(8,128)(2,1)S(1)} %get-tuple-element.113), channel_id=1, source_target_pairs={{0,2},{1,3},{2,0},{3,1},{4,6},{5,7},{6,4},{7,5},{8,10},{9,11},{10,... | collective-permute-start | bytes 786440 | tf_op jit(solution)/shard_map/ppermute | solution.py:560
  282.0 43.0 %collective-permute-start.47 = (bf16[32,1024]{1,0:T(8,128)(2,1)S(1)}, bf16[32,1024]{1,0:T(8,128)(2,1)S(1)}, u32[]{:S(2)}, u32[]{:S(2)}) collective-permute-start(bf16[32,1024]{1,0:T(8,128)(2,1)S(1)} %get-tuple-element.143), channel_id=1, source_target_pairs={{0,16},{8,24},{16,0},{24,8},{1,17},{9,25},{17,1},{25,9},{2,18},{10... | collective-permute-start | bytes 196616 | tf_op jit(solution)/shard_map/ppermute | solution.py:566
  282.0 43.0 %collective-permute-start.46 = (bf16[32,1024]{1,0:T(8,128)(2,1)S(1)}, bf16[32,1024]{1,0:T(8,128)(2,1)S(1)}, u32[]{:S(2)}, u32[]{:S(2)}) collective-permute-start(bf16[32,1024]{1,0:T(8,128)(2,1)S(1)} %get-tuple-element.141), channel_id=1, source_target_pairs={{0,8},{8,16},{16,24},{24,0},{1,9},{9,17},{17,25},{25,1},{2,10},{10... | collective-permute-start | bytes 196616 | tf_op jit(solution)/shard_map/ppermute | solution.py:566
  284.5 61.7 %collective-permute-start.20 = (bf16[1,832,1024]{2,1,0:T(8,128)(2,1)S(1)}, bf16[1,832,1024]{2,1,0:T(8,128)(2,1)S(1)}, u32[]{:S(2)}, u32[]{:S(2)}) collective-permute-start(bf16[1,832,1024]{2,1,0:T(8,128)(2,1)S(1)} %bitcast.96), channel_id=1, source_target_pairs={{0,8},{8,16},{16,24},{24,0},{1,9},{9,17},{17,25},{25,1},{2,10},{10... | collective-permute-start | bytes 5111816 | tf_op jit(solution)/shard_map/ppermute | solution.py:566
  325.0 72.7 %collective-permute-start.52 = (bf16[512,2048]{1,0:T(8,128)(2,1)S(1)}, bf16[512,2048]{1,0:T(8,128)(2,1)S(1)}, u32[]{:S(2)}, u32[]{:S(2)}) collective-permute-start(bf16[512,2048]{1,0:T(8,128)(2,1)S(1)} %copy-done.16), channel_id=1, source_target_pairs={{0,1},{1,0},{2,3},{3,2},{4,5},{5,4},{6,7},{7,6},{8,9},{9,8},{10,11... | collective-permute-start | bytes 6291464 | tf_op jit(solution)/shard_map/ppermute | solution.py:560
  342.3 13.0 %collective-permute-start.35 = (bf16[128,1536]{1,0:T(8,128)(2,1)S(1)}, bf16[128,1536]{1,0:T(8,128)(2,1)S(1)}, u32[]{:S(2)}, u32[]{:S(2)}) collective-permute-start(bf16[128,1536]{1,0:T(8,128)(2,1)S(1)} %get-tuple-element.111), channel_id=1, source_target_pairs={{0,6},{1,7},{2,4},{3,5},{4,2},{5,3},{6,0},{7,1},{8,14},{9,15},{10,... | collective-permute-start | bytes 1179656 | tf_op jit(solution)/shard_map/ppermute | solution.py:560
  344.0 19.9 %collective-permute-start.34 = (bf16[128,1536]{1,0:T(8,128)(2,1)S(1)}, bf16[128,1536]{1,0:T(8,128)(2,1)S(1)}, u32[]{:S(2)}, u32[]{:S(2)}) collective-permute-start(bf16[128,1536]{1,0:T(8,128)(2,1)S(1)} %get-tuple-element.112), channel_id=1, source_target_pairs={{0,4},{1,5},{2,6},{3,7},{4,0},{5,1},{6,2},{7,3},{8,12},{9,13},{10,... | collective-permute-start | bytes 1179656 | tf_op jit(solution)/shard_map/ppermute | solution.py:560
  345.0 20.0 %collective-permute-start.33 = (bf16[128,1536]{1,0:T(8,128)(2,1)S(1)}, bf16[128,1536]{1,0:T(8,128)(2,1)S(1)}, u32[]{:S(2)}, u32[]{:S(2)}) collective-permute-start(bf16[128,1536]{1,0:T(8,128)(2,1)S(1)} %get-tuple-element.110), channel_id=1, source_target_pairs={{0,2},{1,3},{2,0},{3,1},{4,6},{5,7},{6,4},{7,5},{8,10},{9,11},{10,... | collective-permute-start | bytes 1179656 | tf_op jit(solution)/shard_map/ppermute | solution.py:560
  346.2 24.9 %collective-permute-start.25 = (bf16[128,1536]{1,0:T(8,128)(2,1)S(1)}, bf16[128,1536]{1,0:T(8,128)(2,1)S(1)}, u32[]{:S(2)}, u32[]{:S(2)}) collective-permute-start(bf16[128,1536]{1,0:T(8,128)(2,1)S(1)} %get-tuple-element.108), channel_id=1, source_target_pairs={{0,6},{1,7},{2,4},{3,5},{4,2},{5,3},{6,0},{7,1},{8,14},{9,15},{10,... | collective-permute-start | bytes 1179656 | tf_op jit(solution)/shard_map/ppermute | solution.py:560
  355.3 21.4 %collective-permute-start.24 = (bf16[128,1536]{1,0:T(8,128)(2,1)S(1)}, bf16[128,1536]{1,0:T(8,128)(2,1)S(1)}, u32[]{:S(2)}, u32[]{:S(2)}) collective-permute-start(bf16[128,1536]{1,0:T(8,128)(2,1)S(1)} %get-tuple-element.109), channel_id=1, source_target_pairs={{0,4},{1,5},{2,6},{3,7},{4,0},{5,1},{6,2},{7,3},{8,12},{9,13},{10,... | collective-permute-start | bytes 1179656 | tf_op jit(solution)/shard_map/ppermute | solution.py:560
  363.8 12.9 %collective-permute-start.23 = (bf16[128,1536]{1,0:T(8,128)(2,1)S(1)}, bf16[128,1536]{1,0:T(8,128)(2,1)S(1)}, u32[]{:S(2)}, u32[]{:S(2)}) collective-permute-start(bf16[128,1536]{1,0:T(8,128)(2,1)S(1)} %get-tuple-element.107), channel_id=1, source_target_pairs={{0,2},{1,3},{2,0},{3,1},{4,6},{5,7},{6,4},{7,5},{8,10},{9,11},{10,... | collective-permute-start | bytes 1179656 | tf_op jit(solution)/shard_map/ppermute | solution.py:560
  365.3 15.7 %collective-permute-start.38 = (bf16[32,1536]{1,0:T(8,128)(2,1)S(1)}, bf16[32,1536]{1,0:T(8,128)(2,1)S(1)}, u32[]{:S(2)}, u32[]{:S(2)}) collective-permute-start(bf16[32,1536]{1,0:T(8,128)(2,1)S(1)} %get-tuple-element.139), channel_id=1, source_target_pairs={{0,24},{8,0},{16,8},{24,16},{1,25},{9,1},{17,9},{25,17},{2,26},{10... | collective-permute-start | bytes 294920 | tf_op jit(solution)/shard_map/ppermute | solution.py:566
  381.0 14.6 %collective-permute-start.27 = (bf16[32,1536]{1,0:T(8,128)(2,1)S(1)}, bf16[32,1536]{1,0:T(8,128)(2,1)S(1)}, u32[]{:S(2)}, u32[]{:S(2)}) collective-permute-start(bf16[32,1536]{1,0:T(8,128)(2,1)S(1)} %get-tuple-element.137), channel_id=1, source_target_pairs={{0,16},{8,24},{16,0},{24,8},{1,17},{9,25},{17,1},{25,9},{2,18},{10... | collective-permute-start | bytes 294920 | tf_op jit(solution)/shard_map/ppermute | solution.py:566
  381.0 14.6 %collective-permute-start.26 = (bf16[32,1536]{1,0:T(8,128)(2,1)S(1)}, bf16[32,1536]{1,0:T(8,128)(2,1)S(1)}, u32[]{:S(2)}, u32[]{:S(2)}) collective-permute-start(bf16[32,1536]{1,0:T(8,128)(2,1)S(1)} %get-tuple-element.135), channel_id=1, source_target_pairs={{0,8},{8,16},{16,24},{24,0},{1,9},{9,17},{17,25},{25,1},{2,10},{10... | collective-permute-start | bytes 294920 | tf_op jit(solution)/shard_map/ppermute | solution.py:566
  384.3 14.1 %collective-permute-start.39 = (bf16[32,1536]{1,0:T(8,128)(2,1)S(1)}, bf16[32,1536]{1,0:T(8,128)(2,1)S(1)}, u32[]{:S(2)}, u32[]{:S(2)}) collective-permute-start(bf16[32,1536]{1,0:T(8,128)(2,1)S(1)} %get-tuple-element.103), channel_id=1, source_target_pairs={{0,8},{8,16},{16,24},{24,0},{1,9},{9,17},{17,25},{25,1},{2,10},{10... | collective-permute-start | bytes 294920 | tf_op jit(solution)/shard_map/ppermute | solution.py:566
  384.6 16.3 %collective-permute-start.40 = (bf16[32,1536]{1,0:T(8,128)(2,1)S(1)}, bf16[32,1536]{1,0:T(8,128)(2,1)S(1)}, u32[]{:S(2)}, u32[]{:S(2)}) collective-permute-start(bf16[32,1536]{1,0:T(8,128)(2,1)S(1)} %get-tuple-element.103), channel_id=1, source_target_pairs={{0,16},{8,24},{16,0},{24,8},{1,17},{9,25},{17,1},{25,9},{2,18},{10... | collective-permute-start | bytes 294920 | tf_op jit(solution)/shard_map/ppermute | solution.py:566
  395.6 9.9 %collective-permute-start.29 = (bf16[32,1536]{1,0:T(8,128)(2,1)S(1)}, bf16[32,1536]{1,0:T(8,128)(2,1)S(1)}, u32[]{:S(2)}, u32[]{:S(2)}) collective-permute-start(bf16[32,1536]{1,0:T(8,128)(2,1)S(1)} %get-tuple-element.101), channel_id=1, source_target_pairs={{0,8},{8,16},{16,24},{24,0},{1,9},{9,17},{17,25},{25,1},{2,10},{10... | collective-permute-start | bytes 294920 | tf_op jit(solution)/shard_map/ppermute | solution.py:566
  400.9 15.8 %collective-permute-start.55 = (bf16[128,2048]{1,0:T(8,128)(2,1)S(1)}, bf16[128,2048]{1,0:T(8,128)(2,1)S(1)}, u32[]{:S(2)}, u32[]{:S(2)}) collective-permute-start(bf16[128,2048]{1,0:T(8,128)(2,1)S(1)} %get-tuple-element.105), channel_id=1, source_target_pairs={{0,6},{1,7},{2,4},{3,5},{4,2},{5,3},{6,0},{7,1},{8,14},{9,15},{10,... | collective-permute-start | bytes 1572872 | tf_op jit(solution)/shard_map/ppermute | solution.py:560
  404.0 20.9 %collective-permute-start.54 = (bf16[128,2048]{1,0:T(8,128)(2,1)S(1)}, bf16[128,2048]{1,0:T(8,128)(2,1)S(1)}, u32[]{:S(2)}, u32[]{:S(2)}) collective-permute-start(bf16[128,2048]{1,0:T(8,128)(2,1)S(1)} %get-tuple-element.106), channel_id=1, source_target_pairs={{0,4},{1,5},{2,6},{3,7},{4,0},{5,1},{6,2},{7,3},{8,12},{9,13},{10,... | collective-permute-start | bytes 1572872 | tf_op jit(solution)/shard_map/ppermute | solution.py:560
  405.5 19.4 %collective-permute-start.53 = (bf16[128,2048]{1,0:T(8,128)(2,1)S(1)}, bf16[128,2048]{1,0:T(8,128)(2,1)S(1)}, u32[]{:S(2)}, u32[]{:S(2)}) collective-permute-start(bf16[128,2048]{1,0:T(8,128)(2,1)S(1)} %get-tuple-element.104), channel_id=1, source_target_pairs={{0,2},{1,3},{2,0},{3,1},{4,6},{5,7},{6,4},{7,5},{8,10},{9,11},{10,... | collective-permute-start | bytes 1572872 | tf_op jit(solution)/shard_map/ppermute | solution.py:560
  427.1 11.8 %collective-permute-start.57 = (bf16[32,2048]{1,0:T(8,128)(2,1)S(1)}, bf16[32,2048]{1,0:T(8,128)(2,1)S(1)}, u32[]{:S(2)}, u32[]{:S(2)}) collective-permute-start(bf16[32,2048]{1,0:T(8,128)(2,1)S(1)} %get-tuple-element.126), channel_id=1, source_target_pairs={{0,16},{8,24},{16,0},{24,8},{1,17},{9,25},{17,1},{25,9},{2,18},{10... | collective-permute-start | bytes 393224 | tf_op jit(solution)/shard_map/ppermute | solution.py:566
  427.1 11.8 %collective-permute-start.56 = (bf16[32,2048]{1,0:T(8,128)(2,1)S(1)}, bf16[32,2048]{1,0:T(8,128)(2,1)S(1)}, u32[]{:S(2)}, u32[]{:S(2)}) collective-permute-start(bf16[32,2048]{1,0:T(8,128)(2,1)S(1)} %get-tuple-element.124), channel_id=1, source_target_pairs={{0,8},{8,16},{16,24},{24,0},{1,9},{9,17},{17,25},{25,1},{2,10},{10... | collective-permute-start | bytes 393224 | tf_op jit(solution)/shard_map/ppermute | solution.py:566
  441.3 10.2 %collective-permute-start.60 = (bf16[32,2048]{1,0:T(8,128)(2,1)S(1)}, bf16[32,2048]{1,0:T(8,128)(2,1)S(1)}, u32[]{:S(2)}, u32[]{:S(2)}) collective-permute-start(bf16[32,2048]{1,0:T(8,128)(2,1)S(1)} %get-tuple-element.97), channel_id=1, source_target_pairs={{0,16},{8,24},{16,0},{24,8},{1,17},{9,25},{17,1},{25,9},{2,18},{10... | collective-permute-start | bytes 393224 | tf_op jit(solution)/shard_map/ppermute | solution.py:566
  (44 other events, 494.9 us)
